TPU v7x, 256 devices: a whole 4x4x8 slice. The times are simulated.
256 devices in a mesh: dp: 16 (over z, y_lo), blk: 16 (over y_hi, x, core).
Axes of the slice: x: 4, y: 4 (y_hi: 2, y_lo: 2; y = y_hi * 2 + y_lo), z: 8, core: 2. Of those that a mesh axis runs over, the one named last changes fastest.
Arguments:
- images: bfloat16 [98304, 1152], P(('dp', 'blk')), may hold values from -0.1875 to 0.1875
- texts: bfloat16 [32768, 1152], P(('dp', 'blk')), may hold values from -0.1875 to 0.1875
- owners: int32 [98304, 1], P(('dp', 'blk')), may hold values from 0 to 15; in each aligned block of 384 rows (0 to 383, 384 to 767, ...) at most 48 rows name the same one
- labels: int32 [98304], P(('dp', 'blk')), may hold values from 0 to 127
- counts: int32 [256], P(('dp', 'blk')), may hold values from 288 to 384, as said below
- scale: float32 [1], replicated, may hold values from 10 to 30
- bias: float32 [1], replicated, may hold values from -4 to -2
Outputs:
- image_grads: bfloat16 [98304, 1152], P(('dp', 'blk'))
- row_loss: bfloat16 [98304], P(('dp', 'blk'))
- text_grads: bfloat16 [32768, 1152], P(('dp', 'blk'))
Inputs may be any that keep to these rules, and one draw needn't show every extreme that they name: `owners`: among one device's 384 rows no owner is named by more than 48 rows, a bound that some block reaches. `counts`: the live rows are the first ones of each pack; some pack is full in every draw.
All inputs are finite; a program needn't handle non-finite values.
Results may differ from a plain program's by a relative error of at most 0.0065.
Values may be sent and summed in bfloat16 or wider, within the bound.
A program may use at most 64 MiB of HBM per device.

v0:
```python
import jax
import jax.numpy as jnp
from jax import lax
from jax.sharding import PartitionSpec as P


def shifted(block, axis, distance):
    devices = range(lax.axis_size(axis))
    route = [((i - distance) % len(devices), i) for i in devices]
    return lax.ppermute(block, axis, route)


def normalize(rows):
    wide = rows.astype(jnp.float32)
    inv = lax.rsqrt(jnp.sum(wide * wide, axis=1, keepdims=True) + 1e-06)
    return (wide * inv, inv)


def unnormalize(unit, inv, grad):
    return (inv * (grad - unit * jnp.sum(unit * grad, axis=1, keepdims=True))).astype(jnp.bfloat16)


def weigh(units, block, wanted, present, hit, temper, offset):
    logits = (
        temper
        * lax.dot_general(
            units, block, (((1,), (1,)), ((), ())), preferred_element_type=jnp.float32
        )
        + offset
    )
    columns = lax.broadcasted_iota(jnp.int32, logits.shape, 1)
    positive = (columns == wanted[:, None]) & present[:, None] & hit
    sign = jnp.where(positive, 1.0, -1.0).astype(jnp.float32)
    margin = sign * logits
    weight = jnp.where(present[:, None], 1.0, 0.0).astype(jnp.float32)
    losses = jnp.sum(jax.nn.softplus(-margin) * weight, axis=1)
    coef = (-sign * jax.nn.sigmoid(-margin) * temper * weight).astype(jnp.bfloat16)
    return (losses, coef)


def pass_grad(partial_sum):
    return shifted(partial_sum, "blk", 1)


def body(images, texts, owners, labels, counts, scale, bias):
    depth = lax.axis_size("dp")
    cycle = lax.axis_size("blk")
    pack, width = images.shape
    text_rows = texts.shape[0]
    capacity = 2 * pack // depth
    slot_count = depth * capacity
    temper = scale[0]
    offset = bias[0]
    live = jnp.arange(pack, dtype=jnp.int32) < counts[0]
    target_owner = owners[:, 0]
    onehot = (
        (target_owner[:, None] == jnp.arange(depth, dtype=jnp.int32)[None, :]) & live[:, None]
    ).astype(jnp.bfloat16)
    earlier = (jnp.arange(pack)[:, None] > jnp.arange(pack)[None, :]).astype(jnp.bfloat16)
    before = jnp.dot(earlier, onehot, preferred_element_type=jnp.float32)
    place = jnp.sum(before * onehot.astype(jnp.float32), axis=1).astype(jnp.int32)
    target = target_owner * capacity + place
    placed = jnp.where(live, target, slot_count)
    source_row = (
        jnp.zeros((slot_count,), jnp.int32)
        .at[placed]
        .set(jnp.arange(pack, dtype=jnp.int32), mode="drop")
    )
    filled = jnp.zeros((slot_count,), jnp.int32).at[placed].set(1, mode="drop") > 0
    outgoing = jnp.where(filled[:, None], images[source_row], jnp.zeros((), jnp.bfloat16))
    outgoing_tags = jnp.where(filled, labels[source_row] + 1, 0)
    arrived = lax.all_to_all(
        outgoing.reshape(depth, capacity, width), "dp", split_axis=0, concat_axis=0, tiled=True
    ).reshape(slot_count, width)
    arrived_tags = lax.all_to_all(
        outgoing_tags.reshape(depth, capacity), "dp", split_axis=0, concat_axis=0, tiled=True
    ).reshape(slot_count)
    present = arrived_tags > 0
    wanted = arrived_tags - 1
    units, inv = normalize(arrived)
    unit_b = units.astype(jnp.bfloat16)
    text_units, text_inv = normalize(texts)
    text_b = text_units.astype(jnp.bfloat16)

    def turn(step, carry):
        block, partial_sum, image_sum, loss_sum = carry
        losses, coef = weigh(unit_b, block, wanted, present, step == 0, temper, offset)
        image_part = jnp.dot(coef, block, preferred_element_type=jnp.float32)
        text_part = lax.dot_general(
            coef, unit_b, (((0,), (0,)), ((), ())), preferred_element_type=jnp.float32
        )
        moved = pass_grad(partial_sum + text_part)
        block = shifted(block, "blk", 1)
        return (block, moved, image_sum + image_part, loss_sum + losses)

    start = (
        text_b,
        jnp.zeros((text_rows, width), jnp.float32),
        jnp.zeros((slot_count, width), jnp.float32),
        jnp.zeros((slot_count,), jnp.float32),
    )
    block, partial_sum, image_sum, loss_sum = lax.fori_loop(0, cycle - 1, turn, start)
    losses, coef = weigh(unit_b, block, wanted, present, jnp.asarray(cycle == 1), temper, offset)
    image_sum = image_sum + jnp.dot(coef, block, preferred_element_type=jnp.float32)
    text_part = lax.dot_general(
        coef, unit_b, (((0,), (0,)), ((), ())), preferred_element_type=jnp.float32
    )
    text_sum = pass_grad(partial_sum + text_part)
    loss_sum = loss_sum + losses
    image_out = unnormalize(units, inv, image_sum)
    loss_out = (loss_sum / (cycle * text_rows)).astype(jnp.bfloat16)
    back_grads, back_loss = (
        lax.all_to_all(
            image_out.reshape(depth, capacity, width), "dp", split_axis=0, concat_axis=0, tiled=True
        ),
        lax.all_to_all(
            loss_out.reshape(depth, capacity), "dp", split_axis=0, concat_axis=0, tiled=True
        ),
    )
    pick = jnp.where(live, target, 0)
    pack_grads = jnp.where(
        live[:, None], back_grads.reshape(slot_count, width)[pick], jnp.zeros((), jnp.bfloat16)
    )
    pack_loss = jnp.where(live, back_loss.reshape(slot_count)[pick], jnp.zeros((), jnp.bfloat16))
    return (pack_grads, pack_loss, unnormalize(text_units, text_inv, text_sum))


def solution(mesh):
    placed = (
        P(("dp", "blk"), None),
        P(("dp", "blk"), None),
        P(("dp", "blk"), None),
        P(("dp", "blk")),
        P(("dp", "blk")),
        P(),
        P(),
    )
    return jax.shard_map(
        body,
        mesh=mesh,
        in_specs=placed,
        out_specs=(P(("dp", "blk"), None), P(("dp", "blk")), P(("dp", "blk"), None)),
        check_vma=False,
    )
```

profile of v0, /device:TPU:39, one launch (start us, length us, event | category | flops | bytes accessed | tf_op | source)
XLA Modules:
  0.0 456.3 jit_solution(16279595481887000286)
XLA Ops:
  9.5 4.8 %gather_fusion.1 = s32[768]{0:T(1024)S(1)} fusion(s32[384]{0:T(512)} %param.12, s32[1024]{0:T(1024)S(1)} %pad_clamp_fusion.1), kind=kCustom, calls=%fused_computation.1 | custom fusion | bytes 9216 | tf_op jit(solution)/shard_map/gather | solution.py:71
  15.0 9.0 %all-to-all-start.1 = ((s32[16,1,48]{2,1,0:T(1,128)}), s32[16,1,48]{2,1,0:T(1,128)S(1)}, u32[]{:S(2)}, u32[]{:S(2)}) async-start(s32[16,1,48]{2,1,0:T(1,128)} %all_to_all.19), calls=%async_computation.1 | async-start | bytes 16384 | tf_op jit(solution)/shard_map/all_to_all | solution.py:75
  30.2 5.9 %all-to-all-start = ((bf16[16,48,1152]{2,1,0:T(8,128)(2,1)}), bf16[16,48,1152]{2,1,0:T(8,128)(2,1)S(1)}, u32[]{:S(2)}, u32[]{:S(2)}) async-start(bf16[16,48,1152]{2,1,0:T(8,128)(2,1)} %broadcast_select_fusion.1), calls=%async_computation | async-start | bytes 3538944 | tf_op jit(solution)/shard_map/all_to_all | solution.py:72
  39.0 37.1 %all-to-all-done = bf16[16,48,1152]{2,1,0:T(8,128)(2,1)S(1)} async-done(((bf16[16,48,1152]{2,1,0:T(8,128)(2,1)}), bf16[16,48,1152]{2,1,0:T(8,128)(2,1)S(1)}, u32[]{:S(2)}, u32[]{:S(2)}) %all-to-all-start) | async-done | bytes 1769504 | tf_op jit(solution)/shard_map/all_to_all | solution.py:72
  79.1 309.8 %while.20 = (s32[]{:T(128)}, bf16[128,1152]{1,0:T(8,128)(2,1)S(1)}, f32[128,1152]{1,0:T(8,128)}, f32[768,1152]{1,0:T(8,128)}, f32[768]{0:T(1024)S(1)}, /*index=5...) while((s32[]{:T(128)}, bf16[128,1152]{1,0:T(8,128)(2,1)S(1)}, ...), condition=%wide.region_7.8_spmd.clone, body=%wide.region_5.7_spmd.clone.sunk | while | flops 685131264 | bytes 24809724 | solution.py:102
  79.2 4.4 collective-permute-start
  83.5 4.3 fusion.58
  98.1 6.2 %collective-permute-start = (bf16[128,1152]{1,0:T(8,128)(2,1)S(1)}, bf16[128,1152]{1,0:T(8,128)(2,1)S(1)}, u32[]{:S(2)}, u32[]{:S(2)}) collective-permute-start(bf16[128,1152]{1,0:T(8,128)(2,1)S(1)} %copy.17), channel_id=1, source_target_pairs={{15,0},{0,1},{1,2},{2,3},{3,4},{4,5},{5,6},{6,7},{7,8},{8,9},{9,10... | collective-permute-start | bytes 884744 | tf_op jit(solution)/shard_map/while/body/eval_jaxpr/ppermute | solution.py:10
  104.3 4.3 fusion.58
  111.7 5.1 %convolution_add_fusion.7 = f32[768,1152]{1,0:T(8,128)} fusion(bf16[128,1152]{1,0:T(8,128)(2,1)S(1)} %copy.17, f32[768,1152]{1,0:T(8,128)} %get-tuple-element.322, pred[]{:T(512)S(6)} %eq.93, f32[768,128]{0,1:T(8,128)S(1)} %get-tuple-element.305, f32[768]{0:T(1024)S(1)} %broadcast_select_fusion.6, f32[]{:T(128)} %get-tuple-element.338, ...), kind=kOutput, calls=%fused_computation.6.clone.1 | convolution fusion | flops 229343232 | bytes 7772933 | tf_op jit(solution)/shard_map/while/body/eval_jaxpr/dot_general | solution.py:88
  118.9 6.2 %collective-permute-start = (bf16[128,1152]{1,0:T(8,128)(2,1)S(1)}, bf16[128,1152]{1,0:T(8,128)(2,1)S(1)}, u32[]{:S(2)}, u32[]{:S(2)}) collective-permute-start(bf16[128,1152]{1,0:T(8,128)(2,1)S(1)} %copy.17), channel_id=1, source_target_pairs={{15,0},{0,1},{1,2},{2,3},{3,4},{4,5},{5,6},{6,7},{7,8},{8,9},{9,10... | collective-permute-start | bytes 884744 | tf_op jit(solution)/shard_map/while/body/eval_jaxpr/ppermute | solution.py:10
  125.1 4.3 fusion.58
  132.5 5.1 %convolution_add_fusion.7 = f32[768,1152]{1,0:T(8,128)} fusion(bf16[128,1152]{1,0:T(8,128)(2,1)S(1)} %copy.17, f32[768,1152]{1,0:T(8,128)} %get-tuple-element.322, pred[]{:T(512)S(6)} %eq.93, f32[768,128]{0,1:T(8,128)S(1)} %get-tuple-element.305, f32[768]{0:T(1024)S(1)} %broadcast_select_fusion.6, f32[]{:T(128)} %get-tuple-element.338, ...), kind=kOutput, calls=%fused_computation.6.clone.1 | convolution fusion | flops 229343232 | bytes 7772933 | tf_op jit(solution)/shard_map/while/body/eval_jaxpr/dot_general | solution.py:88
  139.7 6.2 %collective-permute-start = (bf16[128,1152]{1,0:T(8,128)(2,1)S(1)}, bf16[128,1152]{1,0:T(8,128)(2,1)S(1)}, u32[]{:S(2)}, u32[]{:S(2)}) collective-permute-start(bf16[128,1152]{1,0:T(8,128)(2,1)S(1)} %copy.17), channel_id=1, source_target_pairs={{15,0},{0,1},{1,2},{2,3},{3,4},{4,5},{5,6},{6,7},{7,8},{8,9},{9,10... | collective-permute-start | bytes 884744 | tf_op jit(solution)/shard_map/while/body/eval_jaxpr/ppermute | solution.py:10
  145.9 4.3 fusion.58
  153.3 5.1 %convolution_add_fusion.7 = f32[768,1152]{1,0:T(8,128)} fusion(bf16[128,1152]{1,0:T(8,128)(2,1)S(1)} %copy.17, f32[768,1152]{1,0:T(8,128)} %get-tuple-element.322, pred[]{:T(512)S(6)} %eq.93, f32[768,128]{0,1:T(8,128)S(1)} %get-tuple-element.305, f32[768]{0:T(1024)S(1)} %broadcast_select_fusion.6, f32[]{:T(128)} %get-tuple-element.338, ...), kind=kOutput, calls=%fused_computation.6.clone.1 | convolution fusion | flops 229343232 | bytes 7772933 | tf_op jit(solution)/shard_map/while/body/eval_jaxpr/dot_general | solution.py:88
  160.5 6.2 %collective-permute-start = (bf16[128,1152]{1,0:T(8,128)(2,1)S(1)}, bf16[128,1152]{1,0:T(8,128)(2,1)S(1)}, u32[]{:S(2)}, u32[]{:S(2)}) collective-permute-start(bf16[128,1152]{1,0:T(8,128)(2,1)S(1)} %copy.17), channel_id=1, source_target_pairs={{15,0},{0,1},{1,2},{2,3},{3,4},{4,5},{5,6},{6,7},{7,8},{8,9},{9,10... | collective-permute-start | bytes 884744 | tf_op jit(solution)/shard_map/while/body/eval_jaxpr/ppermute | solution.py:10
  174.1 5.1 %convolution_add_fusion.7 = f32[768,1152]{1,0:T(8,128)} fusion(bf16[128,1152]{1,0:T(8,128)(2,1)S(1)} %copy.17, f32[768,1152]{1,0:T(8,128)} %get-tuple-element.322, pred[]{:T(512)S(6)} %eq.93, f32[768,128]{0,1:T(8,128)S(1)} %get-tuple-element.305, f32[768]{0:T(1024)S(1)} %broadcast_select_fusion.6, f32[]{:T(128)} %get-tuple-element.338, ...), kind=kOutput, calls=%fused_computation.6.clone.1 | convolution fusion | flops 229343232 | bytes 7772933 | tf_op jit(solution)/shard_map/while/body/eval_jaxpr/dot_general | solution.py:88
  181.2 6.2 %collective-permute-start = (bf16[128,1152]{1,0:T(8,128)(2,1)S(1)}, bf16[128,1152]{1,0:T(8,128)(2,1)S(1)}, u32[]{:S(2)}, u32[]{:S(2)}) collective-permute-start(bf16[128,1152]{1,0:T(8,128)(2,1)S(1)} %copy.17), channel_id=1, source_target_pairs={{15,0},{0,1},{1,2},{2,3},{3,4},{4,5},{5,6},{6,7},{7,8},{8,9},{9,10... | collective-permute-start | bytes 884744 | tf_op jit(solution)/shard_map/while/body/eval_jaxpr/ppermute | solution.py:10
  194.8 5.1 %convolution_add_fusion.7 = f32[768,1152]{1,0:T(8,128)} fusion(bf16[128,1152]{1,0:T(8,128)(2,1)S(1)} %copy.17, f32[768,1152]{1,0:T(8,128)} %get-tuple-element.322, pred[]{:T(512)S(6)} %eq.93, f32[768,128]{0,1:T(8,128)S(1)} %get-tuple-element.305, f32[768]{0:T(1024)S(1)} %broadcast_select_fusion.6, f32[]{:T(128)} %get-tuple-element.338, ...), kind=kOutput, calls=%fused_computation.6.clone.1 | convolution fusion | flops 229343232 | bytes 7772933 | tf_op jit(solution)/shard_map/while/body/eval_jaxpr/dot_general | solution.py:88
  202.0 6.2 %collective-permute-start = (bf16[128,1152]{1,0:T(8,128)(2,1)S(1)}, bf16[128,1152]{1,0:T(8,128)(2,1)S(1)}, u32[]{:S(2)}, u32[]{:S(2)}) collective-permute-start(bf16[128,1152]{1,0:T(8,128)(2,1)S(1)} %copy.17), channel_id=1, source_target_pairs={{15,0},{0,1},{1,2},{2,3},{3,4},{4,5},{5,6},{6,7},{7,8},{8,9},{9,10... | collective-permute-start | bytes 884744 | tf_op jit(solution)/shard_map/while/body/eval_jaxpr/ppermute | solution.py:10
  208.2 4.3 fusion.58
  215.6 5.1 %convolution_add_fusion.7 = f32[768,1152]{1,0:T(8,128)} fusion(bf16[128,1152]{1,0:T(8,128)(2,1)S(1)} %copy.17, f32[768,1152]{1,0:T(8,128)} %get-tuple-element.322, pred[]{:T(512)S(6)} %eq.93, f32[768,128]{0,1:T(8,128)S(1)} %get-tuple-element.305, f32[768]{0:T(1024)S(1)} %broadcast_select_fusion.6, f32[]{:T(128)} %get-tuple-element.338, ...), kind=kOutput, calls=%fused_computation.6.clone.1 | convolution fusion | flops 229343232 | bytes 7772933 | tf_op jit(solution)/shard_map/while/body/eval_jaxpr/dot_general | solution.py:88
  222.8 6.2 %collective-permute-start = (bf16[128,1152]{1,0:T(8,128)(2,1)S(1)}, bf16[128,1152]{1,0:T(8,128)(2,1)S(1)}, u32[]{:S(2)}, u32[]{:S(2)}) collective-permute-start(bf16[128,1152]{1,0:T(8,128)(2,1)S(1)} %copy.17), channel_id=1, source_target_pairs={{15,0},{0,1},{1,2},{2,3},{3,4},{4,5},{5,6},{6,7},{7,8},{8,9},{9,10... | collective-permute-start | bytes 884744 | tf_op jit(solution)/shard_map/while/body/eval_jaxpr/ppermute | solution.py:10
  229.0 4.3 fusion.58
  236.4 5.1 %convolution_add_fusion.7 = f32[768,1152]{1,0:T(8,128)} fusion(bf16[128,1152]{1,0:T(8,128)(2,1)S(1)} %copy.17, f32[768,1152]{1,0:T(8,128)} %get-tuple-element.322, pred[]{:T(512)S(6)} %eq.93, f32[768,128]{0,1:T(8,128)S(1)} %get-tuple-element.305, f32[768]{0:T(1024)S(1)} %broadcast_select_fusion.6, f32[]{:T(128)} %get-tuple-element.338, ...), kind=kOutput, calls=%fused_computation.6.clone.1 | convolution fusion | flops 229343232 | bytes 7772933 | tf_op jit(solution)/shard_map/while/body/eval_jaxpr/dot_general | solution.py:88
  243.6 6.2 %collective-permute-start = (bf16[128,1152]{1,0:T(8,128)(2,1)S(1)}, bf16[128,1152]{1,0:T(8,128)(2,1)S(1)}, u32[]{:S(2)}, u32[]{:S(2)}) collective-permute-start(bf16[128,1152]{1,0:T(8,128)(2,1)S(1)} %copy.17), channel_id=1, source_target_pairs={{15,0},{0,1},{1,2},{2,3},{3,4},{4,5},{5,6},{6,7},{7,8},{8,9},{9,10... | collective-permute-start | bytes 884744 | tf_op jit(solution)/shard_map/while/body/eval_jaxpr/ppermute | solution.py:10
  249.7 4.3 fusion.58
  257.2 5.1 %convolution_add_fusion.7 = f32[768,1152]{1,0:T(8,128)} fusion(bf16[128,1152]{1,0:T(8,128)(2,1)S(1)} %copy.17, f32[768,1152]{1,0:T(8,128)} %get-tuple-element.322, pred[]{:T(512)S(6)} %eq.93, f32[768,128]{0,1:T(8,128)S(1)} %get-tuple-element.305, f32[768]{0:T(1024)S(1)} %broadcast_select_fusion.6, f32[]{:T(128)} %get-tuple-element.338, ...), kind=kOutput, calls=%fused_computation.6.clone.1 | convolution fusion | flops 229343232 | bytes 7772933 | tf_op jit(solution)/shard_map/while/body/eval_jaxpr/dot_general | solution.py:88
  264.3 6.2 %collective-permute-start = (bf16[128,1152]{1,0:T(8,128)(2,1)S(1)}, bf16[128,1152]{1,0:T(8,128)(2,1)S(1)}, u32[]{:S(2)}, u32[]{:S(2)}) collective-permute-start(bf16[128,1152]{1,0:T(8,128)(2,1)S(1)} %copy.17), channel_id=1, source_target_pairs={{15,0},{0,1},{1,2},{2,3},{3,4},{4,5},{5,6},{6,7},{7,8},{8,9},{9,10... | collective-permute-start | bytes 884744 | tf_op jit(solution)/shard_map/while/body/eval_jaxpr/ppermute | solution.py:10
  277.9 5.1 %convolution_add_fusion.7 = f32[768,1152]{1,0:T(8,128)} fusion(bf16[128,1152]{1,0:T(8,128)(2,1)S(1)} %copy.17, f32[768,1152]{1,0:T(8,128)} %get-tuple-element.322, pred[]{:T(512)S(6)} %eq.93, f32[768,128]{0,1:T(8,128)S(1)} %get-tuple-element.305, f32[768]{0:T(1024)S(1)} %broadcast_select_fusion.6, f32[]{:T(128)} %get-tuple-element.338, ...), kind=kOutput, calls=%fused_computation.6.clone.1 | convolution fusion | flops 229343232 | bytes 7772933 | tf_op jit(solution)/shard_map/while/body/eval_jaxpr/dot_general | solution.py:88
  285.1 6.2 %collective-permute-start = (bf16[128,1152]{1,0:T(8,128)(2,1)S(1)}, bf16[128,1152]{1,0:T(8,128)(2,1)S(1)}, u32[]{:S(2)}, u32[]{:S(2)}) collective-permute-start(bf16[128,1152]{1,0:T(8,128)(2,1)S(1)} %copy.17), channel_id=1, source_target_pairs={{15,0},{0,1},{1,2},{2,3},{3,4},{4,5},{5,6},{6,7},{7,8},{8,9},{9,10... | collective-permute-start | bytes 884744 | tf_op jit(solution)/shard_map/while/body/eval_jaxpr/ppermute | solution.py:10
  298.7 5.1 %convolution_add_fusion.7 = f32[768,1152]{1,0:T(8,128)} fusion(bf16[128,1152]{1,0:T(8,128)(2,1)S(1)} %copy.17, f32[768,1152]{1,0:T(8,128)} %get-tuple-element.322, pred[]{:T(512)S(6)} %eq.93, f32[768,128]{0,1:T(8,128)S(1)} %get-tuple-element.305, f32[768]{0:T(1024)S(1)} %broadcast_select_fusion.6, f32[]{:T(128)} %get-tuple-element.338, ...), kind=kOutput, calls=%fused_computation.6.clone.1 | convolution fusion | flops 229343232 | bytes 7772933 | tf_op jit(solution)/shard_map/while/body/eval_jaxpr/dot_general | solution.py:88
  305.9 6.2 %collective-permute-start = (bf16[128,1152]{1,0:T(8,128)(2,1)S(1)}, bf16[128,1152]{1,0:T(8,128)(2,1)S(1)}, u32[]{:S(2)}, u32[]{:S(2)}) collective-permute-start(bf16[128,1152]{1,0:T(8,128)(2,1)S(1)} %copy.17), channel_id=1, source_target_pairs={{15,0},{0,1},{1,2},{2,3},{3,4},{4,5},{5,6},{6,7},{7,8},{8,9},{9,10... | collective-permute-start | bytes 884744 | tf_op jit(solution)/shard_map/while/body/eval_jaxpr/ppermute | solution.py:10
  319.5 5.1 %convolution_add_fusion.7 = f32[768,1152]{1,0:T(8,128)} fusion(bf16[128,1152]{1,0:T(8,128)(2,1)S(1)} %copy.17, f32[768,1152]{1,0:T(8,128)} %get-tuple-element.322, pred[]{:T(512)S(6)} %eq.93, f32[768,128]{0,1:T(8,128)S(1)} %get-tuple-element.305, f32[768]{0:T(1024)S(1)} %broadcast_select_fusion.6, f32[]{:T(128)} %get-tuple-element.338, ...), kind=kOutput, calls=%fused_computation.6.clone.1 | convolution fusion | flops 229343232 | bytes 7772933 | tf_op jit(solution)/shard_map/while/body/eval_jaxpr/dot_general | solution.py:88
  326.7 6.2 %collective-permute-start = (bf16[128,1152]{1,0:T(8,128)(2,1)S(1)}, bf16[128,1152]{1,0:T(8,128)(2,1)S(1)}, u32[]{:S(2)}, u32[]{:S(2)}) collective-permute-start(bf16[128,1152]{1,0:T(8,128)(2,1)S(1)} %copy.17), channel_id=1, source_target_pairs={{15,0},{0,1},{1,2},{2,3},{3,4},{4,5},{5,6},{6,7},{7,8},{8,9},{9,10... | collective-permute-start | bytes 884744 | tf_op jit(solution)/shard_map/while/body/eval_jaxpr/ppermute | solution.py:10
  340.3 5.1 %convolution_add_fusion.7 = f32[768,1152]{1,0:T(8,128)} fusion(bf16[128,1152]{1,0:T(8,128)(2,1)S(1)} %copy.17, f32[768,1152]{1,0:T(8,128)} %get-tuple-element.322, pred[]{:T(512)S(6)} %eq.93, f32[768,128]{0,1:T(8,128)S(1)} %get-tuple-element.305, f32[768]{0:T(1024)S(1)} %broadcast_select_fusion.6, f32[]{:T(128)} %get-tuple-element.338, ...), kind=kOutput, calls=%fused_computation.6.clone.1 | convolution fusion | flops 229343232 | bytes 7772933 | tf_op jit(solution)/shard_map/while/body/eval_jaxpr/dot_general | solution.py:88
  347.4 6.2 %collective-permute-start = (bf16[128,1152]{1,0:T(8,128)(2,1)S(1)}, bf16[128,1152]{1,0:T(8,128)(2,1)S(1)}, u32[]{:S(2)}, u32[]{:S(2)}) collective-permute-start(bf16[128,1152]{1,0:T(8,128)(2,1)S(1)} %copy.17), channel_id=1, source_target_pairs={{15,0},{0,1},{1,2},{2,3},{3,4},{4,5},{5,6},{6,7},{7,8},{8,9},{9,10... | collective-permute-start | bytes 884744 | tf_op jit(solution)/shard_map/while/body/eval_jaxpr/ppermute | solution.py:10
  353.6 4.3 fusion.58
  361.0 5.1 %convolution_add_fusion.7 = f32[768,1152]{1,0:T(8,128)} fusion(bf16[128,1152]{1,0:T(8,128)(2,1)S(1)} %copy.17, f32[768,1152]{1,0:T(8,128)} %get-tuple-element.322, pred[]{:T(512)S(6)} %eq.93, f32[768,128]{0,1:T(8,128)S(1)} %get-tuple-element.305, f32[768]{0:T(1024)S(1)} %broadcast_select_fusion.6, f32[]{:T(128)} %get-tuple-element.338, ...), kind=kOutput, calls=%fused_computation.6.clone.1 | convolution fusion | flops 229343232 | bytes 7772933 | tf_op jit(solution)/shard_map/while/body/eval_jaxpr/dot_general | solution.py:88
  368.2 6.2 %collective-permute-start = (bf16[128,1152]{1,0:T(8,128)(2,1)S(1)}, bf16[128,1152]{1,0:T(8,128)(2,1)S(1)}, u32[]{:S(2)}, u32[]{:S(2)}) collective-permute-start(bf16[128,1152]{1,0:T(8,128)(2,1)S(1)} %copy.17), channel_id=1, source_target_pairs={{15,0},{0,1},{1,2},{2,3},{3,4},{4,5},{5,6},{6,7},{7,8},{8,9},{9,10... | collective-permute-start | bytes 884744 | tf_op jit(solution)/shard_map/while/body/eval_jaxpr/ppermute | solution.py:10
  374.4 4.3 fusion.58
  381.8 5.1 %convolution_add_fusion.7 = f32[768,1152]{1,0:T(8,128)} fusion(bf16[128,1152]{1,0:T(8,128)(2,1)S(1)} %copy.17, f32[768,1152]{1,0:T(8,128)} %get-tuple-element.322, pred[]{:T(512)S(6)} %eq.93, f32[768,128]{0,1:T(8,128)S(1)} %get-tuple-element.305, f32[768]{0:T(1024)S(1)} %broadcast_select_fusion.6, f32[]{:T(128)} %get-tuple-element.338, ...), kind=kOutput, calls=%fused_computation.6.clone.1 | convolution fusion | flops 229343232 | bytes 7772933 | tf_op jit(solution)/shard_map/while/body/eval_jaxpr/dot_general | solution.py:88
  392.6 6.1 %all-to-all-start.3 = ((bf16[16,1,48]{2,1,0:T(2,128)(2,1)}), bf16[16,1,48]{2,1,0:T(2,128)(2,1)S(1)}, u32[]{:S(2)}, u32[]{:S(2)}) async-start(bf16[16,1,48]{2,1,0:T(2,128)(2,1)} %all_to_all.24), calls=%async_computation.3 | async-start | bytes 16384 | tf_op jit(solution)/shard_map/all_to_all | solution.py:116
  404.9 6.5 %all-to-all-start.2 = ((bf16[16,48,1152]{2,1,0:T(8,128)(2,1)}), bf16[16,48,1152]{2,1,0:T(8,128)(2,1)S(1)}, u32[]{:S(2)}, u32[]{:S(2)}) async-start(bf16[16,48,1152]{2,1,0:T(8,128)(2,1)} %bitcast.39), calls=%async_computation.2 | async-start | bytes 3538944 | tf_op jit(solution)/shard_map/all_to_all | solution.py:113
  414.3 7.0 %collective-permute-start.2 = (f32[128,1152]{1,0:T(8,128)}, f32[128,1152]{1,0:T(8,128)}, u32[]{:S(2)}, u32[]{:S(2)}) collective-permute-start(f32[128,1152]{1,0:T(8,128)} %convolution_add_fusion.3), channel_id=1, source_target_pairs={{15,0},{0,1},{1,2},{2,3},{3,4},{4,5},{5,6},{6,7},{7,8},{8,9},{9,10... | collective-permute-start | bytes 1769480 | tf_op jit(solution)/shard_map/ppermute | solution.py:10
  424.8 4.3 collective-permute-done.2
  432.4 20.5 %all-to-all-done.2 = bf16[16,48,1152]{2,1,0:T(8,128)(2,1)S(1)} async-done(((bf16[16,48,1152]{2,1,0:T(8,128)(2,1)}), bf16[16,48,1152]{2,1,0:T(8,128)(2,1)S(1)}, u32[]{:S(2)}, u32[]{:S(2)}) %all-to-all-start.2) | async-done | bytes 1769504 | tf_op jit(solution)/shard_map/all_to_all | solution.py:113
  (212 shorter events, 150.4 us)
Async XLA Ops:
  0.6 23.5 %copy-start = (bf16[384,1152]{1,0:T(8,128)(2,1)S(1)}, bf16[384,1152]{1,0:T(8,128)(2,1)}, u32[]{:S(2)}) copy-start(bf16[384,1152]{1,0:T(8,128)(2,1)} %param.9) | copy-start | bytes 2654212
  15.0 15.2 %all-to-all-start.1 = ((s32[16,1,48]{2,1,0:T(1,128)}), s32[16,1,48]{2,1,0:T(1,128)S(1)}, u32[]{:S(2)}, u32[]{:S(2)}) async-start(s32[16,1,48]{2,1,0:T(1,128)} %all_to_all.19), calls=%async_computation.1 | async-start | bytes 16384 | tf_op jit(solution)/shard_map/all_to_all | solution.py:75
  27.0 10.4 %copy-start.1 = (bf16[128,1152]{1,0:T(8,128)(2,1)S(1)}, bf16[128,1152]{1,0:T(8,128)(2,1)}, u32[]{:S(2)}) copy-start(bf16[128,1152]{1,0:T(8,128)(2,1)} %param.10) | copy-start | bytes 884740
  30.2 45.9 %all-to-all-start = ((bf16[16,48,1152]{2,1,0:T(8,128)(2,1)}), bf16[16,48,1152]{2,1,0:T(8,128)(2,1)S(1)}, u32[]{:S(2)}, u32[]{:S(2)}) async-start(bf16[16,48,1152]{2,1,0:T(8,128)(2,1)} %broadcast_select_fusion.1), calls=%async_computation | async-start | bytes 3538944 | tf_op jit(solution)/shard_map/all_to_all | solution.py:72
  79.2 15.7 %collective-permute-start = (bf16[128,1152]{1,0:T(8,128)(2,1)S(1)}, bf16[128,1152]{1,0:T(8,128)(2,1)S(1)}, u32[]{:S(2)}, u32[]{:S(2)}) collective-permute-start(bf16[128,1152]{1,0:T(8,128)(2,1)S(1)} %copy.17), channel_id=1, source_target_pairs={{15,0},{0,1},{1,2},{2,3},{3,4},{4,5},{5,6},{6,7},{7,8},{8,9},{9,10... | collective-permute-start | bytes 884744 | tf_op jit(solution)/shard_map/while/body/eval_jaxpr/ppermute | solution.py:10
  83.5 4.3 copy-start.2
  90.9 7.2 %collective-permute-start.1 = (f32[128,1152]{1,0:T(8,128)}, f32[128,1152]{1,0:T(8,128)}, u32[]{:S(2)}, u32[]{:S(2)}) collective-permute-start(f32[128,1152]{1,0:T(8,128)} %convolution_add_fusion.6), channel_id=1, source_target_pairs={{15,0},{0,1},{1,2},{2,3},{3,4},{4,5},{5,6},{6,7},{7,8},{8,9},{9,10... | collective-permute-start | bytes 1769480 | tf_op jit(solution)/shard_map/while/body/eval_jaxpr/ppermute | solution.py:10
  98.1 19.4 %collective-permute-start = (bf16[128,1152]{1,0:T(8,128)(2,1)S(1)}, bf16[128,1152]{1,0:T(8,128)(2,1)S(1)}, u32[]{:S(2)}, u32[]{:S(2)}) collective-permute-start(bf16[128,1152]{1,0:T(8,128)(2,1)S(1)} %copy.17), channel_id=1, source_target_pairs={{15,0},{0,1},{1,2},{2,3},{3,4},{4,5},{5,6},{6,7},{7,8},{8,9},{9,10... | collective-permute-start | bytes 884744 | tf_op jit(solution)/shard_map/while/body/eval_jaxpr/ppermute | solution.py:10
  104.3 4.3 copy-start.2
  111.7 7.2 %collective-permute-start.1 = (f32[128,1152]{1,0:T(8,128)}, f32[128,1152]{1,0:T(8,128)}, u32[]{:S(2)}, u32[]{:S(2)}) collective-permute-start(f32[128,1152]{1,0:T(8,128)} %convolution_add_fusion.6), channel_id=1, source_target_pairs={{15,0},{0,1},{1,2},{2,3},{3,4},{4,5},{5,6},{6,7},{7,8},{8,9},{9,10... | collective-permute-start | bytes 1769480 | tf_op jit(solution)/shard_map/while/body/eval_jaxpr/ppermute | solution.py:10
  118.9 19.4 %collective-permute-start = (bf16[128,1152]{1,0:T(8,128)(2,1)S(1)}, bf16[128,1152]{1,0:T(8,128)(2,1)S(1)}, u32[]{:S(2)}, u32[]{:S(2)}) collective-permute-start(bf16[128,1152]{1,0:T(8,128)(2,1)S(1)} %copy.17), channel_id=1, source_target_pairs={{15,0},{0,1},{1,2},{2,3},{3,4},{4,5},{5,6},{6,7},{7,8},{8,9},{9,10... | collective-permute-start | bytes 884744 | tf_op jit(solution)/shard_map/while/body/eval_jaxpr/ppermute | solution.py:10
  132.5 7.2 %collective-permute-start.1 = (f32[128,1152]{1,0:T(8,128)}, f32[128,1152]{1,0:T(8,128)}, u32[]{:S(2)}, u32[]{:S(2)}) collective-permute-start(f32[128,1152]{1,0:T(8,128)} %convolution_add_fusion.6), channel_id=1, source_target_pairs={{15,0},{0,1},{1,2},{2,3},{3,4},{4,5},{5,6},{6,7},{7,8},{8,9},{9,10... | collective-permute-start | bytes 1769480 | tf_op jit(solution)/shard_map/while/body/eval_jaxpr/ppermute | solution.py:10
  139.7 19.4 %collective-permute-start = (bf16[128,1152]{1,0:T(8,128)(2,1)S(1)}, bf16[128,1152]{1,0:T(8,128)(2,1)S(1)}, u32[]{:S(2)}, u32[]{:S(2)}) collective-permute-start(bf16[128,1152]{1,0:T(8,128)(2,1)S(1)} %copy.17), channel_id=1, source_target_pairs={{15,0},{0,1},{1,2},{2,3},{3,4},{4,5},{5,6},{6,7},{7,8},{8,9},{9,10... | collective-permute-start | bytes 884744 | tf_op jit(solution)/shard_map/while/body/eval_jaxpr/ppermute | solution.py:10
  153.3 7.2 %collective-permute-start.1 = (f32[128,1152]{1,0:T(8,128)}, f32[128,1152]{1,0:T(8,128)}, u32[]{:S(2)}, u32[]{:S(2)}) collective-permute-start(f32[128,1152]{1,0:T(8,128)} %convolution_add_fusion.6), channel_id=1, source_target_pairs={{15,0},{0,1},{1,2},{2,3},{3,4},{4,5},{5,6},{6,7},{7,8},{8,9},{9,10... | collective-permute-start | bytes 1769480 | tf_op jit(solution)/shard_map/while/body/eval_jaxpr/ppermute | solution.py:10
  160.5 19.4 %collective-permute-start = (bf16[128,1152]{1,0:T(8,128)(2,1)S(1)}, bf16[128,1152]{1,0:T(8,128)(2,1)S(1)}, u32[]{:S(2)}, u32[]{:S(2)}) collective-permute-start(bf16[128,1152]{1,0:T(8,128)(2,1)S(1)} %copy.17), channel_id=1, source_target_pairs={{15,0},{0,1},{1,2},{2,3},{3,4},{4,5},{5,6},{6,7},{7,8},{8,9},{9,10... | collective-permute-start | bytes 884744 | tf_op jit(solution)/shard_map/while/body/eval_jaxpr/ppermute | solution.py:10
  174.0 7.2 %collective-permute-start.1 = (f32[128,1152]{1,0:T(8,128)}, f32[128,1152]{1,0:T(8,128)}, u32[]{:S(2)}, u32[]{:S(2)}) collective-permute-start(f32[128,1152]{1,0:T(8,128)} %convolution_add_fusion.6), channel_id=1, source_target_pairs={{15,0},{0,1},{1,2},{2,3},{3,4},{4,5},{5,6},{6,7},{7,8},{8,9},{9,10... | collective-permute-start | bytes 1769480 | tf_op jit(solution)/shard_map/while/body/eval_jaxpr/ppermute | solution.py:10
  181.2 19.4 %collective-permute-start = (bf16[128,1152]{1,0:T(8,128)(2,1)S(1)}, bf16[128,1152]{1,0:T(8,128)(2,1)S(1)}, u32[]{:S(2)}, u32[]{:S(2)}) collective-permute-start(bf16[128,1152]{1,0:T(8,128)(2,1)S(1)} %copy.17), channel_id=1, source_target_pairs={{15,0},{0,1},{1,2},{2,3},{3,4},{4,5},{5,6},{6,7},{7,8},{8,9},{9,10... | collective-permute-start | bytes 884744 | tf_op jit(solution)/shard_map/while/body/eval_jaxpr/ppermute | solution.py:10
  187.4 4.3 copy-start.2
  194.8 7.2 %collective-permute-start.1 = (f32[128,1152]{1,0:T(8,128)}, f32[128,1152]{1,0:T(8,128)}, u32[]{:S(2)}, u32[]{:S(2)}) collective-permute-start(f32[128,1152]{1,0:T(8,128)} %convolution_add_fusion.6), channel_id=1, source_target_pairs={{15,0},{0,1},{1,2},{2,3},{3,4},{4,5},{5,6},{6,7},{7,8},{8,9},{9,10... | collective-permute-start | bytes 1769480 | tf_op jit(solution)/shard_map/while/body/eval_jaxpr/ppermute | solution.py:10
  202.0 19.4 %collective-permute-start = (bf16[128,1152]{1,0:T(8,128)(2,1)S(1)}, bf16[128,1152]{1,0:T(8,128)(2,1)S(1)}, u32[]{:S(2)}, u32[]{:S(2)}) collective-permute-start(bf16[128,1152]{1,0:T(8,128)(2,1)S(1)} %copy.17), channel_id=1, source_target_pairs={{15,0},{0,1},{1,2},{2,3},{3,4},{4,5},{5,6},{6,7},{7,8},{8,9},{9,10... | collective-permute-start | bytes 884744 | tf_op jit(solution)/shard_map/while/body/eval_jaxpr/ppermute | solution.py:10
  208.2 4.3 copy-start.2
  215.6 7.2 %collective-permute-start.1 = (f32[128,1152]{1,0:T(8,128)}, f32[128,1152]{1,0:T(8,128)}, u32[]{:S(2)}, u32[]{:S(2)}) collective-permute-start(f32[128,1152]{1,0:T(8,128)} %convolution_add_fusion.6), channel_id=1, source_target_pairs={{15,0},{0,1},{1,2},{2,3},{3,4},{4,5},{5,6},{6,7},{7,8},{8,9},{9,10... | collective-permute-start | bytes 1769480 | tf_op jit(solution)/shard_map/while/body/eval_jaxpr/ppermute | solution.py:10
  222.8 19.4 %collective-permute-start = (bf16[128,1152]{1,0:T(8,128)(2,1)S(1)}, bf16[128,1152]{1,0:T(8,128)(2,1)S(1)}, u32[]{:S(2)}, u32[]{:S(2)}) collective-permute-start(bf16[128,1152]{1,0:T(8,128)(2,1)S(1)} %copy.17), channel_id=1, source_target_pairs={{15,0},{0,1},{1,2},{2,3},{3,4},{4,5},{5,6},{6,7},{7,8},{8,9},{9,10... | collective-permute-start | bytes 884744 | tf_op jit(solution)/shard_map/while/body/eval_jaxpr/ppermute | solution.py:10
  236.4 7.2 %collective-permute-start.1 = (f32[128,1152]{1,0:T(8,128)}, f32[128,1152]{1,0:T(8,128)}, u32[]{:S(2)}, u32[]{:S(2)}) collective-permute-start(f32[128,1152]{1,0:T(8,128)} %convolution_add_fusion.6), channel_id=1, source_target_pairs={{15,0},{0,1},{1,2},{2,3},{3,4},{4,5},{5,6},{6,7},{7,8},{8,9},{9,10... | collective-permute-start | bytes 1769480 | tf_op jit(solution)/shard_map/while/body/eval_jaxpr/ppermute | solution.py:10
  243.6 19.4 %collective-permute-start = (bf16[128,1152]{1,0:T(8,128)(2,1)S(1)}, bf16[128,1152]{1,0:T(8,128)(2,1)S(1)}, u32[]{:S(2)}, u32[]{:S(2)}) collective-permute-start(bf16[128,1152]{1,0:T(8,128)(2,1)S(1)} %copy.17), channel_id=1, source_target_pairs={{15,0},{0,1},{1,2},{2,3},{3,4},{4,5},{5,6},{6,7},{7,8},{8,9},{9,10... | collective-permute-start | bytes 884744 | tf_op jit(solution)/shard_map/while/body/eval_jaxpr/ppermute | solution.py:10
  257.1 7.2 %collective-permute-start.1 = (f32[128,1152]{1,0:T(8,128)}, f32[128,1152]{1,0:T(8,128)}, u32[]{:S(2)}, u32[]{:S(2)}) collective-permute-start(f32[128,1152]{1,0:T(8,128)} %convolution_add_fusion.6), channel_id=1, source_target_pairs={{15,0},{0,1},{1,2},{2,3},{3,4},{4,5},{5,6},{6,7},{7,8},{8,9},{9,10... | collective-permute-start | bytes 1769480 | tf_op jit(solution)/shard_map/while/body/eval_jaxpr/ppermute | solution.py:10
  264.3 19.4 %collective-permute-start = (bf16[128,1152]{1,0:T(8,128)(2,1)S(1)}, bf16[128,1152]{1,0:T(8,128)(2,1)S(1)}, u32[]{:S(2)}, u32[]{:S(2)}) collective-permute-start(bf16[128,1152]{1,0:T(8,128)(2,1)S(1)} %copy.17), channel_id=1, source_target_pairs={{15,0},{0,1},{1,2},{2,3},{3,4},{4,5},{5,6},{6,7},{7,8},{8,9},{9,10... | collective-permute-start | bytes 884744 | tf_op jit(solution)/shard_map/while/body/eval_jaxpr/ppermute | solution.py:10
  277.9 7.2 %collective-permute-start.1 = (f32[128,1152]{1,0:T(8,128)}, f32[128,1152]{1,0:T(8,128)}, u32[]{:S(2)}, u32[]{:S(2)}) collective-permute-start(f32[128,1152]{1,0:T(8,128)} %convolution_add_fusion.6), channel_id=1, source_target_pairs={{15,0},{0,1},{1,2},{2,3},{3,4},{4,5},{5,6},{6,7},{7,8},{8,9},{9,10... | collective-permute-start | bytes 1769480 | tf_op jit(solution)/shard_map/while/body/eval_jaxpr/ppermute | solution.py:10
  285.1 19.4 %collective-permute-start = (bf16[128,1152]{1,0:T(8,128)(2,1)S(1)}, bf16[128,1152]{1,0:T(8,128)(2,1)S(1)}, u32[]{:S(2)}, u32[]{:S(2)}) collective-permute-start(bf16[128,1152]{1,0:T(8,128)(2,1)S(1)} %copy.17), channel_id=1, source_target_pairs={{15,0},{0,1},{1,2},{2,3},{3,4},{4,5},{5,6},{6,7},{7,8},{8,9},{9,10... | collective-permute-start | bytes 884744 | tf_op jit(solution)/shard_map/while/body/eval_jaxpr/ppermute | solution.py:10
  298.7 7.2 %collective-permute-start.1 = (f32[128,1152]{1,0:T(8,128)}, f32[128,1152]{1,0:T(8,128)}, u32[]{:S(2)}, u32[]{:S(2)}) collective-permute-start(f32[128,1152]{1,0:T(8,128)} %convolution_add_fusion.6), channel_id=1, source_target_pairs={{15,0},{0,1},{1,2},{2,3},{3,4},{4,5},{5,6},{6,7},{7,8},{8,9},{9,10... | collective-permute-start | bytes 1769480 | tf_op jit(solution)/shard_map/while/body/eval_jaxpr/ppermute | solution.py:10
  305.9 19.4 %collective-permute-start = (bf16[128,1152]{1,0:T(8,128)(2,1)S(1)}, bf16[128,1152]{1,0:T(8,128)(2,1)S(1)}, u32[]{:S(2)}, u32[]{:S(2)}) collective-permute-start(bf16[128,1152]{1,0:T(8,128)(2,1)S(1)} %copy.17), channel_id=1, source_target_pairs={{15,0},{0,1},{1,2},{2,3},{3,4},{4,5},{5,6},{6,7},{7,8},{8,9},{9,10... | collective-permute-start | bytes 884744 | tf_op jit(solution)/shard_map/while/body/eval_jaxpr/ppermute | solution.py:10
  312.1 4.3 copy-start.2
  319.5 7.2 %collective-permute-start.1 = (f32[128,1152]{1,0:T(8,128)}, f32[128,1152]{1,0:T(8,128)}, u32[]{:S(2)}, u32[]{:S(2)}) collective-permute-start(f32[128,1152]{1,0:T(8,128)} %convolution_add_fusion.6), channel_id=1, source_target_pairs={{15,0},{0,1},{1,2},{2,3},{3,4},{4,5},{5,6},{6,7},{7,8},{8,9},{9,10... | collective-permute-start | bytes 1769480 | tf_op jit(solution)/shard_map/while/body/eval_jaxpr/ppermute | solution.py:10
  326.7 19.4 %collective-permute-start = (bf16[128,1152]{1,0:T(8,128)(2,1)S(1)}, bf16[128,1152]{1,0:T(8,128)(2,1)S(1)}, u32[]{:S(2)}, u32[]{:S(2)}) collective-permute-start(bf16[128,1152]{1,0:T(8,128)(2,1)S(1)} %copy.17), channel_id=1, source_target_pairs={{15,0},{0,1},{1,2},{2,3},{3,4},{4,5},{5,6},{6,7},{7,8},{8,9},{9,10... | collective-permute-start | bytes 884744 | tf_op jit(solution)/shard_map/while/body/eval_jaxpr/ppermute | solution.py:10
  332.8 4.3 copy-start.2
  340.2 7.2 %collective-permute-start.1 = (f32[128,1152]{1,0:T(8,128)}, f32[128,1152]{1,0:T(8,128)}, u32[]{:S(2)}, u32[]{:S(2)}) collective-permute-start(f32[128,1152]{1,0:T(8,128)} %convolution_add_fusion.6), channel_id=1, source_target_pairs={{15,0},{0,1},{1,2},{2,3},{3,4},{4,5},{5,6},{6,7},{7,8},{8,9},{9,10... | collective-permute-start | bytes 1769480 | tf_op jit(solution)/shard_map/while/body/eval_jaxpr/ppermute | solution.py:10
  347.4 19.4 %collective-permute-start = (bf16[128,1152]{1,0:T(8,128)(2,1)S(1)}, bf16[128,1152]{1,0:T(8,128)(2,1)S(1)}, u32[]{:S(2)}, u32[]{:S(2)}) collective-permute-start(bf16[128,1152]{1,0:T(8,128)(2,1)S(1)} %copy.17), channel_id=1, source_target_pairs={{15,0},{0,1},{1,2},{2,3},{3,4},{4,5},{5,6},{6,7},{7,8},{8,9},{9,10... | collective-permute-start | bytes 884744 | tf_op jit(solution)/shard_map/while/body/eval_jaxpr/ppermute | solution.py:10
  361.0 7.2 %collective-permute-start.1 = (f32[128,1152]{1,0:T(8,128)}, f32[128,1152]{1,0:T(8,128)}, u32[]{:S(2)}, u32[]{:S(2)}) collective-permute-start(f32[128,1152]{1,0:T(8,128)} %convolution_add_fusion.6), channel_id=1, source_target_pairs={{15,0},{0,1},{1,2},{2,3},{3,4},{4,5},{5,6},{6,7},{7,8},{8,9},{9,10... | collective-permute-start | bytes 1769480 | tf_op jit(solution)/shard_map/while/body/eval_jaxpr/ppermute | solution.py:10
  368.2 19.4 %collective-permute-start = (bf16[128,1152]{1,0:T(8,128)(2,1)S(1)}, bf16[128,1152]{1,0:T(8,128)(2,1)S(1)}, u32[]{:S(2)}, u32[]{:S(2)}) collective-permute-start(bf16[128,1152]{1,0:T(8,128)(2,1)S(1)} %copy.17), channel_id=1, source_target_pairs={{15,0},{0,1},{1,2},{2,3},{3,4},{4,5},{5,6},{6,7},{7,8},{8,9},{9,10... | collective-permute-start | bytes 884744 | tf_op jit(solution)/shard_map/while/body/eval_jaxpr/ppermute | solution.py:10
  381.8 7.2 %collective-permute-start.1 = (f32[128,1152]{1,0:T(8,128)}, f32[128,1152]{1,0:T(8,128)}, u32[]{:S(2)}, u32[]{:S(2)}) collective-permute-start(f32[128,1152]{1,0:T(8,128)} %convolution_add_fusion.6), channel_id=1, source_target_pairs={{15,0},{0,1},{1,2},{2,3},{3,4},{4,5},{5,6},{6,7},{7,8},{8,9},{9,10... | collective-permute-start | bytes 1769480 | tf_op jit(solution)/shard_map/while/body/eval_jaxpr/ppermute | solution.py:10
  389.0 9.7 %copy-start.5 = (f32[768]{0:T(1024)S(1)}, f32[768]{0:T(1024)}, u32[]{:S(2)}) copy-start(f32[768]{0:T(1024)} %copy-done.4) | copy-start | bytes 9220
  389.0 9.7 %copy-start.6 = (f32[768]{0:T(1024)S(1)}, f32[768]{0:T(1024)}, u32[]{:S(2)}) copy-start(f32[768]{0:T(1024)} %broadcast_select_fusion.3) | copy-start | bytes 9220
  392.6 12.3 %all-to-all-start.3 = ((bf16[16,1,48]{2,1,0:T(2,128)(2,1)}), bf16[16,1,48]{2,1,0:T(2,128)(2,1)S(1)}, u32[]{:S(2)}, u32[]{:S(2)}) async-start(bf16[16,1,48]{2,1,0:T(2,128)(2,1)} %all_to_all.24), calls=%async_computation.3 | async-start | bytes 16384 | tf_op jit(solution)/shard_map/all_to_all | solution.py:116
  403.7 7.8 %copy-start.3 = (f32[768,128]{0,1:T(8,128)S(1)}, f32[768,128]{0,1:T(8,128)}, u32[]{:S(2)}) copy-start(f32[768,128]{0,1:T(8,128)} %get-tuple-element.241) | copy-start | bytes 1179652
  403.7 17.6 %copy-start.7 = (s32[384]{0:T(512)S(1)}, s32[384]{0:T(512)}, u32[]{:S(2)}) copy-start(s32[384]{0:T(512)} %get-tuple-element.212) | copy-start | bytes 4612
  404.9 24.2 %copy-start.9 = (f32[128]{0:T(128)S(1)}, f32[128]{0:T(128)}, u32[]{:S(2)}) copy-start(f32[128]{0:T(128)} %copy-done.8) | copy-start | bytes 1540
  404.9 48.0 %all-to-all-start.2 = ((bf16[16,48,1152]{2,1,0:T(8,128)(2,1)}), bf16[16,48,1152]{2,1,0:T(8,128)(2,1)S(1)}, u32[]{:S(2)}, u32[]{:S(2)}) async-start(bf16[16,48,1152]{2,1,0:T(8,128)(2,1)} %bitcast.39), calls=%async_computation.2 | async-start | bytes 3538944 | tf_op jit(solution)/shard_map/all_to_all | solution.py:113
  414.3 14.8 %collective-permute-start.2 = (f32[128,1152]{1,0:T(8,128)}, f32[128,1152]{1,0:T(8,128)}, u32[]{:S(2)}, u32[]{:S(2)}) collective-permute-start(f32[128,1152]{1,0:T(8,128)} %convolution_add_fusion.3), channel_id=1, source_target_pairs={{15,0},{0,1},{1,2},{2,3},{3,4},{4,5},{5,6},{6,7},{7,8},{8,9},{9,10... | collective-permute-start | bytes 1769480 | tf_op jit(solution)/shard_map/ppermute | solution.py:10
  (13 other events, 46.4 us)
where the time goes:
time: 462 us; the launch traced here: 456 us
  matrix products  195 us (42%)
  starting transfers between devices  126 us (27%)
  waiting for transfers between devices  86.5 us (19%)
  other arithmetic  23.8 us (5%)
  local copies, waits for them, and re-layouts  22.2 us (5%)
    ppermute x31, starting transfers between devices, shifted(): return lax.ppermute(block, axis, route)  98.3 us
    dot_general x15, matrix products, turn(): image_part = jnp.dot(coef, block, preferred_element_type=jnp.float32)  75.2 us
    dot_general x16, matrix products, weigh(): lax.dot_general(units, block, (((1,), (1,)), ((), ())), preferred_element...  67.9 us
    dot_general x15, matrix products, turn(): lax.dot_general(coef, unit_b, (((0,), (0,)), ((), ())), preferred_element...  45.9 us
    all_to_all x1, waiting for transfers between devices, body(): lax.all_to_all(outgoing.reshape(depth, capacity, width), 'dp', split_axis...  37.1 us
    ppermute x31, waiting for transfers between devices, shifted(): return lax.ppermute(block, axis, route)  26 us
    all_to_all x1, waiting for transfers between devices, body(): lax.all_to_all(image_out.reshape(depth, capacity, width), 'dp', split_axi...  20.5 us
    add x15, other arithmetic, turn(): return (block, moved, image_sum + image_part, loss_sum + losses)  10.3 us
  transfers between devices with their start and end apart: 35, of which 20 were waited for; matrix products, arithmetic and copies ran while one was open for 47% of the time, Pallas kernels for 0%

commit v1 on v0

v1 whole, which is shorter than its diff:
```python
import functools

import jax
import jax.numpy as jnp
from jax import lax
from jax.experimental import pallas as pl
from jax.experimental.pallas import tpu as pltpu
from jax.sharding import PartitionSpec as P

MESH = pl.DeviceIdType.MESH
BF16 = jnp.bfloat16
F32 = jnp.float32
EPS = 1e-06

NZ, NY, NH, NX = 8, 2, 2, 4
PACK = 384
ROWS = 128
CAP = 48
BUCKETS = 16
SLOTS = CAP * BUCKETS
WIDTH = 1152
TEXTS = 2048
GROUP = 256
GROUPS = SLOTS // GROUP
TILE = 512
TILES = TEXTS // TILE

ORDER = (
    (4, 0), (4, 1), (3, 0), (5, 0), (3, 1),
    (5, 1), (2, 0), (6, 0), (2, 1), (6, 1),
    (1, 0), (7, 0), (1, 1), (7, 1), (0, 1), (0, 0),
)
SELF = BUCKETS - 1


def place_of():
    p, c = lax.axis_index("dp"), lax.axis_index("blk")
    return p // NY, p % NY, c // (2 * NX), (c // 2) % NX, c % 2


def peer(dz=0, dy=0, dh=0, dx=0, dc=0):
    z, y, h, x, core = place_of()
    return (
        ((z + dz) % NZ) * NY + (y + dy) % NY,
        (((h + dh) % NH) * NX + (x + dx) % NX) * 2 + (core + dc) % 2,
    )


def block_index(dh, dx, dc):
    return (dh * NX + dx) * 2 + dc


def dot(a, b, dims):
    return lax.dot_general(a, b, ((dims[:1], dims[1:]), ((), ())), preferred_element_type=F32)


def spread():
    lane = lax.broadcasted_iota(jnp.int32, (128, SLOTS), 1)
    row = lax.broadcasted_iota(jnp.int32, (128, SLOTS), 0)
    return jnp.where(lane % CAP == row, 1.0, 0.0).astype(BF16)


def own_lanes(every):
    lane = lax.broadcasted_iota(jnp.int32, (128, SLOTS), 1)
    row = lax.broadcasted_iota(jnp.int32, (128, SLOTS), 0)
    own = lane // CAP == row // 8
    return own if every else own & (row % 8 == 0)


def pack_row(row, spreader):
    kept = jnp.where(own_lanes(True), row, 0.0).astype(BF16)
    return dot(kept, spreader, (1, 1)).reshape(BUCKETS, 8, 128)


def unpack_row(tiles, spreader):
    wide = dot(tiles.reshape(128, 128).astype(BF16), spreader, (1, 0))
    return jnp.sum(jnp.where(own_lanes(False), wide, 0.0), axis=0, keepdims=True)


def kernel(
    img_ref, txt_ref, own_ref, lab_ref, cnt_ref, scale_ref, bias_ref,
    grad_ref, loss_ref, tgrad_ref,
    pick_ref, out_ref, recv_ref, unit_ref, gsend_ref, back_ref,
    tagsend_ref, tagrecv_ref, losssend_ref, lossback_ref,
    texts_ref, tsum_ref, isum_ref, lsum_ref, inv_ref,
    sibsend_ref, sibrecv_ref, xsend_ref, xrecv_ref, ysend_ref, yrecv_ref,
    img_sems, tag_sems, back_sems, lback_sems, txt_sems, sib_sems, x_sems, y_sems,
):
    temper, offset, live_rows = scale_ref[0], bias_ref[0], cnt_ref[0]

    barrier = pltpu.get_barrier_semaphore()
    greeted = [peer(dz=dz, dy=dy) for dz, dy in ORDER[:SELF]]
    greeted += [peer(dc=1), peer(dh=1), peer(dx=1), peer(dx=2), peer(dx=3)]
    for device in greeted:
        pl.semaphore_signal(barrier, inc=1, device_id=device, device_id_type=MESH)

    def remote(src, dst, sems, index, device):
        return pltpu.make_async_remote_copy(
            src_ref=src,
            dst_ref=dst,
            send_sem=sems.at[0, index],
            recv_sem=sems.at[1, index],
            device_id=device,
            device_id_type=MESH,
        )

    bucket = lax.broadcasted_iota(jnp.int32, (BUCKETS, PACK), 0)
    owner_of = jnp.zeros((BUCKETS, PACK), jnp.int32)
    for o, (dz, dy) in enumerate(ORDER):
        owner_of = jnp.where(bucket == o, peer(dz=dz, dy=dy)[0], owner_of)
    live = lax.broadcasted_iota(jnp.int32, (BUCKETS, PACK), 1) < live_rows
    onehot = jnp.where((own_ref[...] == owner_of) & live, 1.0, 0.0)
    earlier = jnp.where(
        lax.broadcasted_iota(jnp.int32, (PACK, PACK), 0)
        < lax.broadcasted_iota(jnp.int32, (PACK, PACK), 1),
        1.0,
        0.0,
    ).astype(BF16)
    before = dot(onehot.astype(BF16), earlier, (1, 0))
    target = jnp.sum(onehot * (before + (bucket * CAP + 1).astype(F32)), axis=0, keepdims=True)
    target = target.astype(jnp.int32) - 1
    slot = lax.broadcasted_iota(jnp.int32, (SLOTS, PACK), 0)
    pick_ref[...] = jnp.where(slot == target, 1.0, 0.0).astype(BF16)
    spreader = spread()
    tags = dot(
        jnp.broadcast_to((lab_ref[...] + 1).astype(F32), (8, PACK)).astype(BF16), pick_ref[...], (1, 1)
    )
    tagsend_ref[...] = pack_row(tags[0:1], spreader)
    tagrecv_ref[SELF] = tagsend_ref[SELF]

    img_copies = [
        remote(
            out_ref.at[pl.ds(CAP * o, CAP)], recv_ref.at[pl.ds(CAP * o, CAP)], img_sems, o,
            peer(dz=ORDER[o][0], dy=ORDER[o][1]),
        )
        for o in range(SELF)
    ]
    tag_copies = [
        remote(
            tagsend_ref.at[o], tagrecv_ref.at[o], tag_sems, o, peer(dz=ORDER[o][0], dy=ORDER[o][1])
        )
        for o in range(SELF)
    ]
    pl.semaphore_wait(barrier, len(greeted))
    for copy in tag_copies:
        copy.start()
    for g in range(GROUPS):
        rows = pl.ds(g * GROUP, GROUP)
        out_ref[rows, :] = dot(pick_ref[rows, :], img_ref[...], (1, 0)).astype(BF16)
        for o in range(BUCKETS):
            end = (o + 1) * CAP
            if g * GROUP < end <= (g + 1) * GROUP and o != SELF:
                img_copies[o].start()
    kept = pl.ds(SELF * CAP, CAP)
    recv_ref[kept, :] = out_ref[kept, :]

    wide = txt_ref[...].astype(F32)
    texts_ref[pl.ds(0, ROWS), :] = (
        wide * lax.rsqrt(jnp.sum(wide * wide, axis=1, keepdims=True) + EPS)
    ).astype(BF16)

    def text_copy(dh, dx, dc):
        if dc:
            source, device = (dh, dx, 0), peer(dc=1)
        elif dx:
            source, device = (dh, 0, 0), peer(dx=-dx)
        else:
            source, device = (0, 0, 0), peer(dh=1)
        j, i = block_index(dh, dx, dc), block_index(*source)
        return remote(
            texts_ref.at[pl.ds(ROWS * i, ROWS)], texts_ref.at[pl.ds(ROWS * j, ROWS)], txt_sems, j, device
        )

    near = (1, 3, 2)
    text_copies = {
        (dh, dx, dc): text_copy(dh, dx, dc)
        for dh in range(NH)
        for dx in range(NX)
        for dc in range(2)
        if (dh, dx, dc) != (0, 0, 0)
    }
    text_copies[1, 0, 0].start()
    for dx in near:
        text_copies[0, dx, 0].start()
    text_copies[0, 0, 1].start()
    text_copies[1, 0, 0].wait_recv()
    for dx in near:
        text_copies[1, dx, 0].start()
    text_copies[1, 0, 1].start()
    for dh in range(NH):
        for dx in near:
            text_copies[dh, dx, 0].wait_recv()
            text_copies[dh, dx, 1].start()
    for dh in range(NH):
        for dx in range(NX):
            text_copies[dh, dx, 1].wait_recv()

    for copy in tag_copies:
        copy.wait_recv()
    wanted = unpack_row(tagrecv_ref[...], spreader).astype(jnp.int32) - 1

    back_copies = [
        remote(
            gsend_ref.at[pl.ds(CAP * o, CAP)], back_ref.at[pl.ds(CAP * o, CAP)], back_sems, o,
            peer(dz=-ORDER[o][0], dy=ORDER[o][1]),
        )
        for o in range(SELF)
    ]
    lback_copies = [
        remote(
            losssend_ref.at[o], lossback_ref.at[o], lback_sems, o, peer(dz=-ORDER[o][0], dy=ORDER[o][1])
        )
        for o in range(SELF)
    ]

    arrived = 0
    for g in range(GROUPS):
        rows = pl.ds(g * GROUP, GROUP)
        while arrived < SELF and arrived * CAP < (g + 1) * GROUP:
            img_copies[arrived].wait_recv()
            arrived += 1
        wide = recv_ref[rows, :].astype(F32)
        inv = lax.rsqrt(jnp.sum(wide * wide, axis=1, keepdims=True) + EPS)
        inv_ref[...] = inv
        unit_ref[...] = (wide * inv).astype(BF16)
        isum_ref[...] = jnp.zeros_like(isum_ref)
        lsum_ref[...] = jnp.zeros_like(lsum_ref)
        hit = wanted[:, g * GROUP : (g + 1) * GROUP]

        def turn(t, carry, g=g, hit=hit):
            part = pl.ds(pl.multiple_of(t * TILE, TILE), TILE)
            block = texts_ref[part, :]
            unit = unit_ref[...]
            logit = temper * dot(block, unit, (1, 1)) + offset
            text = lax.broadcasted_iota(jnp.int32, logit.shape, 0) + t * TILE
            positive = text == hit
            m = jnp.where(positive, -logit, logit)
            e = jnp.exp(-jnp.abs(m))
            one = 1.0 + e
            series = e * (1.0 - e * (0.5 - e * (1.0 / 3.0)))
            log1p = jnp.where(e < 0.015625, series, jnp.log(one))
            lsum_ref[...] += jnp.sum(jnp.maximum(m, 0.0) + log1p, axis=0, keepdims=True)
            sigmoid = jnp.where(m >= 0.0, 1.0, e) / one
            coef = (jnp.where(positive, -temper, temper) * sigmoid).astype(BF16)
            text_part = dot(coef, unit, (1, 0))
            if g == 0:
                tsum_ref[part, :] = text_part
            else:
                tsum_ref[part, :] += text_part
            isum_ref[...] += dot(coef, block, (0, 0))
            return carry

        lax.fori_loop(0, TILES, turn, 0)

        image_sum = isum_ref[...]
        inv = inv_ref[...]
        unit = recv_ref[rows, :].astype(F32) * inv
        along = jnp.sum(unit * image_sum, axis=1, keepdims=True)
        gsend_ref[rows, :] = (inv * (image_sum - unit * along)).astype(BF16)
        row = (lsum_ref[...] / TEXTS).astype(BF16).astype(F32)
        parts = [jnp.zeros((1, GROUP), F32)] * GROUPS
        parts[g] = row
        if g == 0:
            losses = jnp.concatenate(parts, axis=1)
        else:
            losses = losses + jnp.concatenate(parts, axis=1)
        done = [o for o in range(BUCKETS) if g * GROUP < (o + 1) * CAP <= (g + 1) * GROUP]
        tiles = pack_row(losses, spreader)
        losssend_ref[pl.ds(done[0], len(done))] = tiles[done[0] : done[-1] + 1]
        for o in done:
            if o != SELF:
                back_copies[o].start()
                lback_copies[o].start()
    back_ref[kept, :] = gsend_ref[kept, :]
    lossback_ref[SELF] = losssend_ref[SELF]

    def block(ref, dh, dx, dc):
        return ref[pl.ds(ROWS * block_index(dh, dx, dc), ROWS), :]

    def pair(dh, dx):
        return dh * NX + dx

    far = (1, 3, 2, 0)
    sib_copies = {}
    for dh in (1, 0):
        for dx in far:
            k = pair(dh, dx)
            sibsend_ref[k] = block(tsum_ref, dh, dx, 1).astype(BF16)
            sib_copies[k] = remote(sibsend_ref.at[k], sibrecv_ref.at[k], sib_sems, k, peer(dc=1))
            sib_copies[k].start()
    x_copies = {}
    for dh in (1, 0):
        for dx in far:
            k = pair(dh, dx)
            sib_copies[k].wait_recv()
            total = block(tsum_ref, dh, dx, 0) + sibrecv_ref[k].astype(F32)
            if dx == 0:
                tsum_ref[pl.ds(ROWS * block_index(dh, 0, 0), ROWS), :] = total
            else:
                xsend_ref[k] = total.astype(BF16)
                x_copies[k] = remote(xsend_ref.at[k], xrecv_ref.at[k], x_sems, k, peer(dx=dx))
                x_copies[k].start()

    def gathered(dh):
        total = block(tsum_ref, dh, 0, 0)
        for dx in (1, 3, 2):
            x_copies[pair(dh, dx)].wait_recv()
            total = total + xrecv_ref[pair(dh, dx)].astype(F32)
        return total

    ysend_ref[...] = gathered(1).astype(BF16)
    y_copy = remote(ysend_ref, yrecv_ref, y_sems, 0, peer(dh=1))
    y_copy.start()
    total = gathered(0)
    y_copy.wait_recv()
    total = total + yrecv_ref[...].astype(F32)
    wide = txt_ref[...].astype(F32)
    inv = lax.rsqrt(jnp.sum(wide * wide, axis=1, keepdims=True) + EPS)
    unit = wide * inv
    along = jnp.sum(unit * total, axis=1, keepdims=True)
    tgrad_ref[...] = (inv * (total - unit * along)).astype(BF16)

    for o in range(SELF):
        back_copies[o].wait_recv()
        lback_copies[o].wait_recv()
    grad_ref[...] = dot(pick_ref[...], back_ref[...], (0, 0)).astype(BF16)
    row = unpack_row(lossback_ref[...], spreader)
    loss_ref[...] = dot(jnp.broadcast_to(row, (8, SLOTS)).astype(BF16), pick_ref[...], (1, 0))[0:1]

    for copies in (img_copies, tag_copies, back_copies, lback_copies):
        for copy in copies:
            copy.wait_send()
    for copies in (text_copies, sib_copies, x_copies):
        for copy in copies.values():
            copy.wait_send()
    y_copy.wait_send()


def body(images, texts, owners, labels, counts, scale, bias):
    vmem = pl.BlockSpec(memory_space=pltpu.VMEM)
    smem = pl.BlockSpec(memory_space=pltpu.SMEM)
    dma = pltpu.SemaphoreType.DMA
    block_rows = (ROWS, WIDTH)
    grads, loss, text_grads = pl.pallas_call(
        kernel,
        out_shape=(
            jax.ShapeDtypeStruct((PACK, WIDTH), BF16),
            jax.ShapeDtypeStruct((1, PACK), F32),
            jax.ShapeDtypeStruct(block_rows, BF16),
        ),
        in_specs=[vmem] * 4 + [smem] * 3,
        out_specs=(vmem, vmem, vmem),
        scratch_shapes=[
            pltpu.VMEM((SLOTS, PACK), BF16),
            pltpu.VMEM((SLOTS, WIDTH), BF16),
            pltpu.VMEM((SLOTS, WIDTH), BF16),
            pltpu.VMEM((GROUP, WIDTH), BF16),
            pltpu.VMEM((SLOTS, WIDTH), BF16),
            pltpu.VMEM((SLOTS, WIDTH), BF16),
            pltpu.VMEM((BUCKETS, 8, 128), F32),
            pltpu.VMEM((BUCKETS, 8, 128), F32),
            pltpu.VMEM((BUCKETS, 8, 128), F32),
            pltpu.VMEM((BUCKETS, 8, 128), F32),
            pltpu.VMEM((TEXTS, WIDTH), BF16),
            pltpu.VMEM((TEXTS, WIDTH), F32),
            pltpu.VMEM((GROUP, WIDTH), F32),
            pltpu.VMEM((1, GROUP), F32),
            pltpu.VMEM((GROUP, 1), F32),
            pltpu.VMEM((NH * NX,) + block_rows, BF16),
            pltpu.VMEM((NH * NX,) + block_rows, BF16),
            pltpu.VMEM((NH * NX,) + block_rows, BF16),
            pltpu.VMEM((NH * NX,) + block_rows, BF16),
            pltpu.VMEM(block_rows, BF16),
            pltpu.VMEM(block_rows, BF16),
            dma((2, SELF)),
            dma((2, SELF)),
            dma((2, SELF)),
            dma((2, SELF)),
            dma((2, BUCKETS)),
            dma((2, NH * NX)),
            dma((2, NH * NX)),
            dma((2, 1)),
        ],
        compiler_params=pltpu.CompilerParams(
            collective_id=0, has_side_effects=True, vmem_limit_bytes=56 << 20
        ),
    )(images, texts, owners.reshape(1, PACK), labels.reshape(1, PACK), counts, scale, bias)
    return grads, loss.reshape(PACK).astype(BF16), text_grads


def solution(mesh):
    rows = P(("dp", "blk"), None)
    line = P(("dp", "blk"))
    return jax.shard_map(
        body,
        mesh=mesh,
        in_specs=(rows, rows, rows, line, line, P(), P()),
        out_specs=(rows, line, rows),
        check_vma=False,
    )
```

time: 462 us -> 113 us (0.24)
  the two profiles are of different devices: /device:TPU:39 before, /device:TPU:1 now
where the time goes in v1:
time: 113 us
  Pallas kernels  106 us (94%)
  local copies, waits for them, and re-layouts  4.11 us (4%)
  between operations  2.61 us (2%)
    pallas_call x1, Pallas kernels, body(): pl.pallas_call(kernel, out_shape=(jax.ShapeDtypeStruct((PACK, WIDTH), BF1...  106 us
    unnamed x8, local copies, waits for them, and re-layouts  3.55 us

profile of v1, /device:TPU:1, one launch (start us, length us, event | category | flops | bytes accessed | tf_op | source)
XLA Modules:
  0.0 113.2 jit_solution(6581681335509659878)
XLA Ops:
  1.9 0.0 copy-start.1
  2.6 0.0 copy-done.1
  2.6 0.6 reshape.15.lab_ref
  3.2 105.9 %shard_map.94 = (bf16[384,1152]{1,0:T(8,128)(2,1)}, f32[1,384]{1,0:T(1,128)}, bf16[128,1152]{1,0:T(8,128)(2,1)}) custom-call(bf16[384,1152]{1,0:T(8,128)(2,1)} %img_ref.1, bf16[128,1152]{1,0:T(8,128)(2,1)} %txt_ref.1, s32[1,384]{1,0:T(1,128)} %bitcast.1, s32[1,384]{1,0:T(1,128)} %reshape.15.lab_ref, s32[1]{0:T(128)S(6)} %copy.12.cnt_ref, ...), custom_call_target="tpu_custom_call" | custom-call | tf_op jit(solution)/shard_map/pallas_call | solution.py:344
  109.1 0.0 copy-start.2
  109.1 0.6 copy-done.2
  109.7 0.6 convert_reduce_fusion
  110.3 0.0 copy-start
  110.3 2.2 %copy.15 = bf16[384,1152]{1,0:T(8,128)(2,1)} copy(bf16[384,1152]{1,0:T(8,128)(2,1)} %get-tuple-element.12) | data formatting | bytes 1769472
  112.5 0.0 copy-done
  112.5 0.7 copy.16
Async XLA Ops:
  1.9 0.7 copy-start.1
  109.1 0.6 copy-start.2
  110.3 2.2 %copy-start = (bf16[128,1152]{1,0:T(8,128)(2,1)S(1)}, bf16[128,1152]{1,0:T(8,128)(2,1)}, u32[]{:S(2)}) copy-start(bf16[128,1152]{1,0:T(8,128)(2,1)} %get-tuple-element.14) | copy-start | bytes 884740

commit v2 on v1

v2 whole, which is shorter than its diff:
```python
import functools

import jax
import jax.numpy as jnp
from jax import lax
from jax.experimental import pallas as pl
from jax.experimental.pallas import tpu as pltpu
from jax.sharding import PartitionSpec as P

MESH = pl.DeviceIdType.MESH
BF16 = jnp.bfloat16
F32 = jnp.float32
EPS = 1e-06

NZ, NY, NH, NX = 8, 2, 2, 4
PACK = 384
ROWS = 128
CAP = 48
BUCKETS = 16
SLOTS = CAP * BUCKETS
WIDTH = 1152
TEXTS = 2048
GROUP = 256
GROUPS = SLOTS // GROUP
HALF = ROWS // 2
COLUMNS = 1152

ORDER = (
    (0, 0), (0, 1), (1, 0), (7, 0), (1, 1), (7, 1),
    (2, 0), (6, 0), (2, 1), (6, 1), (3, 0),
    (5, 0), (3, 1), (5, 1), (4, 0), (4, 1),
)
SENT = range(1, BUCKETS)
EARLY = 10
DRAINED = 5


def place_of():
    p, c = lax.axis_index("dp"), lax.axis_index("blk")
    return p // NY, p % NY, c // (2 * NX), (c // 2) % NX, c % 2


def peer(dz=0, dy=0, dh=0, dx=0, dc=0):
    z, y, h, x, core = place_of()
    return (
        ((z + dz) % NZ) * NY + (y + dy) % NY,
        (((h + dh) % NH) * NX + (x + dx) % NX) * 2 + (core + dc) % 2,
    )


def block_index(dh, dx, dc):
    return (dh * 2 + dc) * NX + dx


def dot(a, b, dims):
    return lax.dot_general(a, b, ((dims[:1], dims[1:]), ((), ())), preferred_element_type=F32)


def spread():
    lane = lax.broadcasted_iota(jnp.int32, (128, SLOTS), 1)
    row = lax.broadcasted_iota(jnp.int32, (128, SLOTS), 0)
    return jnp.where(lane % CAP == row, 1.0, 0.0).astype(BF16)


def own_lanes(every):
    lane = lax.broadcasted_iota(jnp.int32, (128, SLOTS), 1)
    row = lax.broadcasted_iota(jnp.int32, (128, SLOTS), 0)
    own = lane // CAP == row // 8
    return own if every else own & (row % 8 == 0)


def pack_row(row, spreader):
    kept = jnp.where(own_lanes(True), row, 0.0).astype(BF16)
    return dot(kept, spreader, (1, 1)).reshape(BUCKETS, 8, 128)


def unpack_row(tiles, spreader):
    wide = dot(tiles.reshape(128, 128).astype(BF16), spreader, (1, 0))
    return jnp.sum(jnp.where(own_lanes(False), wide, 0.0), axis=0, keepdims=True)


def kernel(
    img_hbm, txt_hbm, own_ref, lab_ref, cnt_ref, scale_ref, bias_ref,
    back_ref, pick_hbm, loss_ref, tgrad_ref,
    img_ref, txt_ref, pick_ref, pick_t_ref, out_ref, recv_ref, unit_ref, coef_ref, gsend_ref,
    tagsend_ref, tagrecv_ref, losssend_ref, lossback_ref,
    texts_ref, tsum_ref, isum_ref,
    sibsend_ref, sibrecv_ref, xsend_ref, xrecv_ref, ysend_ref, yrecv_ref,
    img_sems, tag_sems, back_sems, lback_sems, txt_sems, sib_sems, x_sems, y_sems, local_sems,
):
    temper, offset, live_rows = scale_ref[0], bias_ref[0], cnt_ref[0]

    barrier = pltpu.get_barrier_semaphore()
    greeted = [peer(dz=ORDER[o][0], dy=ORDER[o][1]) for o in SENT]
    greeted += [peer(dc=1), peer(dh=1), peer(dx=1), peer(dx=3)]
    for device in greeted:
        pl.semaphore_signal(barrier, inc=1, device_id=device, device_id_type=MESH)
    img_load = pltpu.make_async_copy(img_hbm, img_ref, local_sems.at[0])
    txt_load = pltpu.make_async_copy(txt_hbm, txt_ref, local_sems.at[1])
    img_load.start()
    txt_load.start()

    def remote(src, dst, sems, index, device):
        return pltpu.make_async_remote_copy(
            src_ref=src,
            dst_ref=dst,
            send_sem=sems.at[0, index],
            recv_sem=sems.at[1, index],
            device_id=device,
            device_id_type=MESH,
        )

    bucket = lax.broadcasted_iota(jnp.int32, (BUCKETS, PACK), 0)
    owner_of = jnp.zeros((BUCKETS, PACK), jnp.int32)
    for o, (dz, dy) in enumerate(ORDER):
        owner_of = jnp.where(bucket == o, peer(dz=dz, dy=dy)[0], owner_of)
    live = lax.broadcasted_iota(jnp.int32, (BUCKETS, PACK), 1) < live_rows
    onehot = jnp.where((own_ref[...] == owner_of) & live, 1.0, 0.0)
    earlier = jnp.where(
        lax.broadcasted_iota(jnp.int32, (PACK, PACK), 0)
        < lax.broadcasted_iota(jnp.int32, (PACK, PACK), 1),
        1.0,
        0.0,
    ).astype(BF16)
    before = dot(onehot.astype(BF16), earlier, (1, 0))
    target = jnp.sum(onehot * (before + (bucket * CAP + 1).astype(F32)), axis=0, keepdims=True)
    target = target.astype(jnp.int32) - 1
    slot = lax.broadcasted_iota(jnp.int32, (SLOTS, PACK), 0)
    pick_ref[...] = jnp.where(slot == target, 1.0, 0.0).astype(BF16)
    spreader = spread()
    tags = dot(
        jnp.broadcast_to((lab_ref[...].reshape(1, PACK) + 1).astype(F32), (8, PACK)).astype(BF16),
        pick_ref[...],
        (1, 1),
    )
    tagsend_ref[...] = pack_row(tags[0:1], spreader)
    tagrecv_ref[0] = tagsend_ref[0]

    def bucket_rows(o):
        return pl.ds(CAP * o, CAP)

    def away(o):
        return peer(dz=ORDER[o][0], dy=ORDER[o][1])

    def home(o):
        return peer(dz=-ORDER[o][0], dy=ORDER[o][1])

    img_copies, tag_copies, back_copies, lback_copies = {}, {}, {}, {}
    for o in SENT:
        rows = bucket_rows(o)
        img_copies[o] = remote(out_ref.at[rows], recv_ref.at[rows], img_sems, o, away(o))
        tag_copies[o] = remote(tagsend_ref.at[o], tagrecv_ref.at[o], tag_sems, o, away(o))
        back_copies[o] = remote(gsend_ref.at[rows], back_ref.at[rows], back_sems, o, home(o))
        lback_copies[o] = remote(losssend_ref.at[o], lossback_ref.at[o], lback_sems, o, home(o))

    img_load.wait()
    out_ref[...] = dot(pick_ref[...], img_ref[...], (1, 0)).astype(BF16)
    txt_load.wait()
    wide = txt_ref[...].astype(F32)
    texts_ref[pl.ds(0, ROWS), :] = (
        wide * lax.rsqrt(jnp.sum(wide * wide, axis=1, keepdims=True) + EPS)
    ).astype(BF16)
    pl.semaphore_wait(barrier, len(greeted))
    for o in SENT[:EARLY]:
        img_copies[o].start()

    def text_rows(dh, dx, dc, first=0, count=ROWS):
        return texts_ref.at[pl.ds(ROWS * block_index(dh, dx, dc) + first, count)]

    text_copies = {}

    def text_send(key, src, dst, device):
        text_copies[key] = remote(src, dst, txt_sems, len(text_copies), device)
        text_copies[key].start()

    def to_sibling(dh, dx):
        text_send(("c", dh, dx), text_rows(dh, dx, 0), text_rows(dh, dx, 1), peer(dc=1))

    def to_neighbours(dh):
        text_send(("x", dh, 3), text_rows(dh, 0, 0), text_rows(dh, 3, 0), peer(dx=1))
        text_send(("x", dh, 1), text_rows(dh, 0, 0), text_rows(dh, 1, 0), peer(dx=3))

    def relay(dh):
        text_copies["x", dh, 3].wait_recv()
        text_send(("r", dh, 0), text_rows(dh, 3, 0, 0, HALF), text_rows(dh, 2, 0, 0, HALF), peer(dx=1))
        to_sibling(dh, 3)
        text_copies["x", dh, 1].wait_recv()
        text_send(
            ("r", dh, 1), text_rows(dh, 1, 0, HALF, HALF), text_rows(dh, 2, 0, HALF, HALF), peer(dx=3)
        )
        to_sibling(dh, 1)

    def relayed(dh):
        text_copies["r", dh, 0].wait_recv()
        text_copies["r", dh, 1].wait_recv()
        to_sibling(dh, 2)

    text_send("h", text_rows(0, 0, 0), text_rows(1, 0, 0), peer(dh=1))
    to_neighbours(0)
    to_sibling(0, 0)
    for o in SENT:
        tag_copies[o].start()
    recv_ref[bucket_rows(0), :] = out_ref[bucket_rows(0), :]
    pick_t_ref[...] = pick_ref[...].T
    pick_save = pltpu.make_async_copy(pick_t_ref, pick_hbm, local_sems.at[0])
    pick_save.start()
    inv, loss_sum, hits, sib_copies = {}, {}, {}, {}
    far = (2, 1, 3, 0)

    def group_rows(g):
        return pl.ds(g * GROUP, GROUP)

    def prepare(g, first, end):
        for o in range(max(first, 1), end):
            img_copies[o].wait_recv()
        wide = recv_ref[group_rows(g), :].astype(F32)
        inv[g] = lax.rsqrt(jnp.sum(wide * wide, axis=1, keepdims=True) + EPS)
        unit_ref[group_rows(g), :] = (wide * inv[g]).astype(BF16)

    def weigh(g, dh):
        half = pl.ds(dh * TEXTS // 2, TEXTS // 2)
        logit = temper * dot(texts_ref[half, :], unit_ref[group_rows(g), :], (1, 1)) + offset
        text = lax.broadcasted_iota(jnp.int32, logit.shape, 0) + dh * TEXTS // 2
        positive = text == hits["all"][:, g * GROUP : (g + 1) * GROUP]
        m = jnp.where(positive, -logit, logit)
        e = jnp.exp(-jnp.abs(m))
        one = 1.0 + e
        series = e * (1.0 - e * (0.5 - e * (1.0 / 3.0)))
        log1p = jnp.where(e < 0.015625, series, jnp.log(one))
        part_sum = jnp.sum(jnp.maximum(m, 0.0) + log1p, axis=0, keepdims=True)
        loss_sum[g] = loss_sum[g] + part_sum if g in loss_sum else part_sum
        sigmoid = jnp.where(m >= 0.0, 1.0, e) / one
        coef_ref[...] = (jnp.where(positive, -temper, temper) * sigmoid).astype(BF16)
        for dc in (1, 0):
            own = pl.ds(dc * TEXTS // 4, TEXTS // 4)
            part = pl.ds((dh * 2 + dc) * TEXTS // 4, TEXTS // 4)
            text_part = dot(coef_ref[own, :], unit_ref[group_rows(g), :], (1, 0))
            if g == 0:
                tsum_ref[part, :] = text_part
            else:
                tsum_ref[part, :] += text_part
            if g == GROUPS - 1 and dc:
                for dx in far:
                    k = dh * NX + dx
                    sibsend_ref[k] = tsum_ref[pl.ds(ROWS * block_index(dh, dx, 1), ROWS), :].astype(BF16)
                    sib_copies[k] = remote(sibsend_ref.at[k], sibrecv_ref.at[k], sib_sems, k, peer(dc=1))
                    sib_copies[k].start()
        image_part = dot(coef_ref[...], texts_ref[half, :], (0, 0))
        if dh == (1 if g == GROUPS - 1 else 0):
            isum_ref[group_rows(g), :] = image_part
        else:
            isum_ref[group_rows(g), :] += image_part

    def project(g):
        image_sum = isum_ref[group_rows(g), :]
        unit = recv_ref[group_rows(g), :].astype(F32) * inv[g]
        along = jnp.sum(unit * image_sum, axis=1, keepdims=True)
        gsend_ref[group_rows(g), :] = (inv[g] * (image_sum - unit * along)).astype(BF16)

    def complete(dh):
        for dx in range(NX):
            text_copies["c", dh, dx].wait_recv()

    relay(0)
    text_copies["h"].wait_recv()
    to_neighbours(1)
    to_sibling(1, 0)
    for o in SENT[:DRAINED]:
        img_copies[o].wait_send()
    for o in SENT[EARLY:]:
        img_copies[o].start()
    relayed(0)
    for o in SENT:
        tag_copies[o].wait_recv()
    hits["all"] = unpack_row(tagrecv_ref[...], spreader).astype(jnp.int32) - 1
    complete(0)
    prepare(0, 0, 6)
    weigh(0, 0)
    relay(1)
    prepare(1, 6, 11)
    weigh(1, 0)
    relayed(1)
    complete(1)
    weigh(0, 1)
    project(0)
    for o in range(1, 5):
        back_copies[o].start()
    weigh(1, 1)
    project(1)
    for o in range(5, 10):
        back_copies[o].start()
    prepare(2, 11, BUCKETS)
    weigh(2, 1)
    weigh(2, 0)
    project(2)
    for o in range(10, BUCKETS):
        back_copies[o].start()
    losses = jnp.concatenate([loss_sum[g] for g in range(GROUPS)], axis=1)
    losses = (losses / TEXTS).astype(BF16).astype(F32)
    losssend_ref[...] = pack_row(losses, spreader)
    keep = pltpu.make_async_copy(
        gsend_ref.at[bucket_rows(0)], back_ref.at[bucket_rows(0)], local_sems.at[1]
    )
    keep.start()
    for o in SENT:
        lback_copies[o].start()
    lossback_ref[0] = losssend_ref[0]

    x_copies = {}

    def x_send(dh, m, value):
        xsend_ref[dh, m] = value.astype(BF16)
        device = peer(dx=3 if m % 2 else 1)
        x_copies[dh, m] = remote(xsend_ref.at[dh, m], xrecv_ref.at[dh, m], x_sems, dh * 6 + m, device)
        x_copies[dh, m].start()

    def x_received(dh, m):
        x_copies[dh, m].wait_recv()
        return xrecv_ref[dh, m].astype(F32)

    def chip_sum(dh, dx):
        k = dh * NX + dx
        sib_copies[k].wait_recv()
        total = tsum_ref[pl.ds(ROWS * block_index(dh, dx, 0), ROWS), :] + sibrecv_ref[k].astype(F32)
        return total[:HALF], total[HALF:]

    kept = {}
    for dh in (1, 0):
        low, high = chip_sum(dh, 2)
        x_send(dh, 0, low)
        x_send(dh, 1, high)
        ahead, high = chip_sum(dh, 1)
        x_send(dh, 2, high)
        low, behind = chip_sum(dh, 3)
        x_send(dh, 3, low)
        kept[dh] = chip_sum(dh, 0)
        x_send(dh, 4, ahead + x_received(dh, 0))
        x_send(dh, 5, behind + x_received(dh, 1))

    def gathered(dh):
        low, high = kept[dh]
        return jnp.concatenate(
            [
                low + x_received(dh, 3) + x_received(dh, 4),
                high + x_received(dh, 2) + x_received(dh, 5),
            ],
            axis=0,
        )

    ysend_ref[...] = gathered(1).astype(BF16)
    y_copy = remote(ysend_ref, yrecv_ref, y_sems, 0, peer(dh=1))
    y_copy.start()
    total = gathered(0)
    y_copy.wait_recv()
    total = total + yrecv_ref[...].astype(F32)
    wide = txt_ref[...].astype(F32)
    inv = lax.rsqrt(jnp.sum(wide * wide, axis=1, keepdims=True) + EPS)
    unit = wide * inv
    along = jnp.sum(unit * total, axis=1, keepdims=True)
    tgrad_ref[...] = (inv * (total - unit * along)).astype(BF16)

    pick_save.wait()
    keep.wait()
    y_copy.wait_send()
    for o in SENT[DRAINED:]:
        img_copies[o].wait_send()
    for copies in (text_copies, tag_copies, sib_copies, x_copies):
        for copy in copies.values():
            copy.wait_send()
    for copy in lback_copies.values():
        copy.wait()
    row = jnp.broadcast_to(unpack_row(lossback_ref[...], spreader), (8, SLOTS)).astype(BF16)
    loss_ref[...] = dot(row, pick_ref[...], (1, 0))[0:1]
    for copy in back_copies.values():
        copy.wait()


def finish(back_ref, pick_ref, losses_ref, sums_ref, grad_ref, loss_ref, tgrad_ref):
    grad_ref[...] = dot(pick_ref[...], back_ref[...], (1, 0)).astype(BF16)
    tgrad_ref[...] = sums_ref[...]
    loss_ref[...] = losses_ref[...].astype(BF16).reshape(PACK)


def body(images, texts, owners, labels, counts, scale, bias):
    vmem = pl.BlockSpec(memory_space=pltpu.VMEM)
    smem = pl.BlockSpec(memory_space=pltpu.SMEM)
    anywhere = pl.BlockSpec(memory_space=pl.ANY)
    dma = pltpu.SemaphoreType.DMA
    blocks = NH * NX
    back, pick, losses, sums = pl.pallas_call(
        kernel,
        out_shape=(
            jax.ShapeDtypeStruct((SLOTS, WIDTH), BF16),
            jax.ShapeDtypeStruct((PACK, SLOTS), BF16),
            jax.ShapeDtypeStruct((1, PACK), F32),
            jax.ShapeDtypeStruct((ROWS, WIDTH), BF16),
        ),
        in_specs=[anywhere] * 2 + [vmem] * 2 + [smem] * 3,
        out_specs=(anywhere, anywhere, vmem, vmem),
        scratch_shapes=[
            pltpu.VMEM((PACK, WIDTH), BF16),
            pltpu.VMEM((ROWS, WIDTH), BF16),
            pltpu.VMEM((SLOTS, PACK), BF16),
            pltpu.VMEM((PACK, SLOTS), BF16),
            pltpu.VMEM((SLOTS, WIDTH), BF16),
            pltpu.VMEM((SLOTS, WIDTH), BF16),
            pltpu.VMEM((SLOTS, WIDTH), BF16),
            pltpu.VMEM((TEXTS // 2, GROUP), BF16),
            pltpu.VMEM((SLOTS, WIDTH), BF16),
            pltpu.VMEM((BUCKETS, 8, 128), F32),
            pltpu.VMEM((BUCKETS, 8, 128), F32),
            pltpu.VMEM((BUCKETS, 8, 128), F32),
            pltpu.VMEM((BUCKETS, 8, 128), F32),
            pltpu.VMEM((TEXTS, WIDTH), BF16),
            pltpu.VMEM((TEXTS, WIDTH), F32),
            pltpu.VMEM((SLOTS, WIDTH), F32),
            pltpu.VMEM((blocks, ROWS, WIDTH), BF16),
            pltpu.VMEM((blocks, ROWS, WIDTH), BF16),
            pltpu.VMEM((NH, 6, HALF, WIDTH), BF16),
            pltpu.VMEM((NH, 6, HALF, WIDTH), BF16),
            pltpu.VMEM((ROWS, WIDTH), BF16),
            pltpu.VMEM((ROWS, WIDTH), BF16),
            dma((2, BUCKETS)),
            dma((2, BUCKETS)),
            dma((2, BUCKETS)),
            dma((2, BUCKETS)),
            dma((2, 17)),
            dma((2, blocks)),
            dma((2, 6 * NH)),
            dma((2, 1)),
            dma((2,)),
        ],
        compiler_params=pltpu.CompilerParams(
            collective_id=0, has_side_effects=True, vmem_limit_bytes=56 << 20
        ),
    )(images, texts, owners.reshape(1, PACK), labels, counts, scale, bias)
    columns = lambda rows: pl.BlockSpec((rows, COLUMNS), lambda i: (0, i))
    grads, loss, text_grads = pl.pallas_call(
        finish,
        grid=(WIDTH // COLUMNS,),
        out_shape=(
            jax.ShapeDtypeStruct((PACK, WIDTH), BF16),
            jax.ShapeDtypeStruct((PACK,), BF16),
            jax.ShapeDtypeStruct((ROWS, WIDTH), BF16),
        ),
        in_specs=[
            columns(SLOTS),
            pl.BlockSpec((PACK, SLOTS), lambda i: (0, 0)),
            pl.BlockSpec((1, PACK), lambda i: (0, 0)),
            columns(ROWS),
        ],
        out_specs=(columns(PACK), pl.BlockSpec((PACK,), lambda i: (0,)), columns(ROWS)),
        compiler_params=pltpu.CompilerParams(vmem_limit_bytes=60 << 20),
    )(back, pick, losses, sums)
    return grads, loss, text_grads


def solution(mesh):
    rows = P(("dp", "blk"), None)
    line = P(("dp", "blk"))
    return jax.shard_map(
        body,
        mesh=mesh,
        in_specs=(rows, rows, rows, line, line, P(), P()),
        out_specs=(rows, line, rows),
        check_vma=False,
    )
```

time: 113 us -> 109 us (0.965)
  the two profiles are of different devices: /device:TPU:1 before, /device:TPU:17 now
where the time goes in v2:
time: 109 us
  Pallas kernels  106 us (97%)
  between operations  2.58 us (2%)
    pallas_call x1, Pallas kernels, body(): pl.pallas_call(kernel, out_shape=(jax.ShapeDtypeStruct((SLOTS, WIDTH), BF...  103 us
    pallas_call x1, Pallas kernels, body(): pl.pallas_call(finish, grid=(WIDTH // COLUMNS,), out_shape=(jax.ShapeDtyp...  3.57 us

profile of v2, /device:TPU:17, one launch (start us, length us, event | category | flops | bytes accessed | tf_op | source)
XLA Modules:
  0.0 108.7 jit_solution(4644888726042833770)
XLA Ops:
  2.6 102.5 %shard_map.94 = (bf16[768,1152]{1,0:T(8,128)(2,1)}, bf16[384,768]{1,0:T(8,128)(2,1)}, f32[1,384]{1,0:T(1,128)}, bf16[128,1152]{1,0:T(8,128)(2,1)}) custom-call(bf16[384,1152]{1,0:T(8,128)(2,1)} %img_hbm.1, bf16[128,1152]{1,0:T(8,128)(2,1)} %txt_hbm.1, s32[1,384]{1,0:T(1,128)} %bitcast.1, s32[384]{0:T(512)} %lab_ref.1, s32[1]{0:T(128)S(6)} %copy.10.cnt_ref, ...), custom_call_target="tpu_custom_call" | custom-call | tf_op jit(solution)/shard_map/pallas_call | solution.py:390
  105.1 3.6 %shard_map.95 = (bf16[384,1152]{1,0:T(8,128)(2,1)}, bf16[384]{0:T(512)(128)(2,1)}, bf16[128,1152]{1,0:T(8,128)(2,1)}) custom-call(bf16[768,1152]{1,0:T(8,128)(2,1)} %get-tuple-element.7.back_ref, bf16[384,768]{1,0:T(8,128)(2,1)} %get-tuple-element.8.pick_ref, f32[1,384]{1,0:T(1,128)} %get-tuple-element.9.losses_ref, bf16[128,1152]{1,0:T(8,128)(2,1)} %get-tuple-element.10.sums_ref), custom_call_target="tpu_custom_call" | custom-call | tf_op jit(solution)/shard_map/pallas_call | solution.py:438

commit v3 on v2

--- a/solution.py
+++ b/solution.py
@@ -31,8 +31,8 @@
     (5, 0), (3, 1), (5, 1), (4, 0), (4, 1),
 )
 SENT = range(1, BUCKETS)
-EARLY = 10
-DRAINED = 5
+BATCHES = (SENT[:7], SENT[7:11], SENT[11:])
+LEFT = (SENT[:4], SENT[4:7], SENT[7:])
 
 
 def place_of():
@@ -161,7 +161,9 @@
         wide * lax.rsqrt(jnp.sum(wide * wide, axis=1, keepdims=True) + EPS)
     ).astype(BF16)
     pl.semaphore_wait(barrier, len(greeted))
-    for o in SENT[:EARLY]:
+    for o in SENT:
+        tag_copies[o].start()
+    for o in BATCHES[0]:
         img_copies[o].start()
 
     def text_rows(dh, dx, dc, first=0, count=ROWS):
@@ -198,8 +200,6 @@
     text_send("h", text_rows(0, 0, 0), text_rows(1, 0, 0), peer(dh=1))
     to_neighbours(0)
     to_sibling(0, 0)
-    for o in SENT:
-        tag_copies[o].start()
     recv_ref[bucket_rows(0), :] = out_ref[bucket_rows(0), :]
     pick_t_ref[...] = pick_ref[...].T
     pick_save = pltpu.make_async_copy(pick_t_ref, pick_hbm, local_sems.at[0])
@@ -261,14 +261,17 @@
         for dx in range(NX):
             text_copies["c", dh, dx].wait_recv()
 
+    def next_batch(i):
+        for o in LEFT[i]:
+            img_copies[o].wait_send()
+        for o in BATCHES[i + 1]:
+            img_copies[o].start()
+
+    next_batch(0)
     relay(0)
     text_copies["h"].wait_recv()
     to_neighbours(1)
     to_sibling(1, 0)
-    for o in SENT[:DRAINED]:
-        img_copies[o].wait_send()
-    for o in SENT[EARLY:]:
-        img_copies[o].start()
     relayed(0)
     for o in SENT:
         tag_copies[o].wait_recv()
@@ -276,6 +279,7 @@
     complete(0)
     prepare(0, 0, 6)
     weigh(0, 0)
+    next_batch(1)
     relay(1)
     prepare(1, 6, 11)
     weigh(1, 0)
@@ -292,19 +296,19 @@
     prepare(2, 11, BUCKETS)
     weigh(2, 1)
     weigh(2, 0)
+    losses = jnp.concatenate([loss_sum[g] for g in range(GROUPS)], axis=1)
+    losses = (losses / TEXTS).astype(BF16).astype(F32)
+    losssend_ref[...] = pack_row(losses, spreader)
+    for o in SENT:
+        lback_copies[o].start()
+    lossback_ref[0] = losssend_ref[0]
     project(2)
     for o in range(10, BUCKETS):
         back_copies[o].start()
-    losses = jnp.concatenate([loss_sum[g] for g in range(GROUPS)], axis=1)
-    losses = (losses / TEXTS).astype(BF16).astype(F32)
-    losssend_ref[...] = pack_row(losses, spreader)
     keep = pltpu.make_async_copy(
         gsend_ref.at[bucket_rows(0)], back_ref.at[bucket_rows(0)], local_sems.at[1]
     )
     keep.start()
-    for o in SENT:
-        lback_copies[o].start()
-    lossback_ref[0] = losssend_ref[0]
 
     x_copies = {}
 
@@ -362,7 +366,7 @@
     pick_save.wait()
     keep.wait()
     y_copy.wait_send()
-    for o in SENT[DRAINED:]:
+    for o in LEFT[2]:
         img_copies[o].wait_send()
     for copies in (text_copies, tag_copies, sib_copies, x_copies):
         for copy in copies.values():

time: 109 us -> 106 us (0.972)
  the two profiles are of different devices: /device:TPU:17 before, /device:TPU:39 now
where the time goes in v3:
time: 106 us; the launch traced here: 105 us
  Pallas kernels  103 us (97%)
  between operations  2.58 us (2%)
    pallas_call x1, Pallas kernels, body(): pl.pallas_call(kernel, out_shape=(jax.ShapeDtypeStruct((SLOTS, WIDTH), BF...  99.3 us
    pallas_call x1, Pallas kernels, body(): pl.pallas_call(finish, grid=(WIDTH // COLUMNS,), out_shape=(jax.ShapeDtyp...  3.56 us

profile of v3, /device:TPU:39, one launch (start us, length us, event | category | flops | bytes accessed | tf_op | source)
XLA Modules:
  0.0 105.4 jit_solution(17005604084922013138)
XLA Ops:
  2.6 99.3 %shard_map.94 = (bf16[768,1152]{1,0:T(8,128)(2,1)}, bf16[384,768]{1,0:T(8,128)(2,1)}, f32[1,384]{1,0:T(1,128)}, bf16[128,1152]{1,0:T(8,128)(2,1)}) custom-call(bf16[384,1152]{1,0:T(8,128)(2,1)} %img_hbm.1, bf16[128,1152]{1,0:T(8,128)(2,1)} %txt_hbm.1, s32[1,384]{1,0:T(1,128)} %bitcast.1, s32[384]{0:T(512)} %lab_ref.1, s32[1]{0:T(128)S(6)} %copy.10.cnt_ref, ...), custom_call_target="tpu_custom_call" | custom-call | tf_op jit(solution)/shard_map/pallas_call | solution.py:394
  101.9 3.6 %shard_map.95 = (bf16[384,1152]{1,0:T(8,128)(2,1)}, bf16[384]{0:T(512)(128)(2,1)}, bf16[128,1152]{1,0:T(8,128)(2,1)}) custom-call(bf16[768,1152]{1,0:T(8,128)(2,1)} %get-tuple-element.7.back_ref, bf16[384,768]{1,0:T(8,128)(2,1)} %get-tuple-element.8.pick_ref, f32[1,384]{1,0:T(1,128)} %get-tuple-element.9.losses_ref, bf16[128,1152]{1,0:T(8,128)(2,1)} %get-tuple-element.10.sums_ref), custom_call_target="tpu_custom_call" | custom-call | tf_op jit(solution)/shard_map/pallas_call | solution.py:442

commit v4 on v3

--- a/solution.py
+++ b/solution.py
@@ -81,10 +81,10 @@
 
 def kernel(
     img_hbm, txt_hbm, own_ref, lab_ref, cnt_ref, scale_ref, bias_ref,
-    back_ref, pick_hbm, loss_ref, tgrad_ref,
+    back_ref, pick_hbm, loss_hbm, tgrad_hbm,
     img_ref, txt_ref, pick_ref, pick_t_ref, out_ref, recv_ref, unit_ref, coef_ref, gsend_ref,
     tagsend_ref, tagrecv_ref, losssend_ref, lossback_ref,
-    texts_ref, tsum_ref, isum_ref,
+    texts_ref, tsum_ref, isum_ref, loss_ref, tgrad_ref,
     sibsend_ref, sibrecv_ref, xsend_ref, xrecv_ref, ysend_ref, yrecv_ref,
     img_sems, tag_sems, back_sems, lback_sems, txt_sems, sib_sems, x_sems, y_sems, local_sems,
 ):
@@ -362,6 +362,8 @@
     unit = wide * inv
     along = jnp.sum(unit * total, axis=1, keepdims=True)
     tgrad_ref[...] = (inv * (total - unit * along)).astype(BF16)
+    tgrad_save = pltpu.make_async_copy(tgrad_ref, tgrad_hbm, local_sems.at[2])
+    tgrad_save.start()
 
     pick_save.wait()
     keep.wait()
@@ -375,6 +377,10 @@
         copy.wait()
     row = jnp.broadcast_to(unpack_row(lossback_ref[...], spreader), (8, SLOTS)).astype(BF16)
     loss_ref[...] = dot(row, pick_ref[...], (1, 0))[0:1]
+    loss_save = pltpu.make_async_copy(loss_ref, loss_hbm, local_sems.at[3])
+    loss_save.start()
+    tgrad_save.wait()
+    loss_save.wait()
     for copy in back_copies.values():
         copy.wait()
 
@@ -400,7 +406,7 @@
             jax.ShapeDtypeStruct((ROWS, WIDTH), BF16),
         ),
         in_specs=[anywhere] * 2 + [vmem] * 2 + [smem] * 3,
-        out_specs=(anywhere, anywhere, vmem, vmem),
+        out_specs=(anywhere,) * 4,
         scratch_shapes=[
             pltpu.VMEM((PACK, WIDTH), BF16),
             pltpu.VMEM((ROWS, WIDTH), BF16),
@@ -418,6 +424,8 @@
             pltpu.VMEM((TEXTS, WIDTH), BF16),
             pltpu.VMEM((TEXTS, WIDTH), F32),
             pltpu.VMEM((SLOTS, WIDTH), F32),
+            pltpu.VMEM((1, PACK), F32),
+            pltpu.VMEM((ROWS, WIDTH), BF16),
             pltpu.VMEM((blocks, ROWS, WIDTH), BF16),
             pltpu.VMEM((blocks, ROWS, WIDTH), BF16),
             pltpu.VMEM((NH, 6, HALF, WIDTH), BF16),
@@ -432,7 +440,7 @@
             dma((2, blocks)),
             dma((2, 6 * NH)),
             dma((2, 1)),
-            dma((2,)),
+            dma((4,)),
         ],
         compiler_params=pltpu.CompilerParams(
             collective_id=0, has_side_effects=True, vmem_limit_bytes=56 << 20

time: 106 us -> 105 us (level)
  no operation moved by 1% of the time
where the time goes in v4:
time: 105 us
  Pallas kernels  102 us (97%)
  between operations  2.58 us (2%)
    pallas_call x1, Pallas kernels, body(): pl.pallas_call(kernel, out_shape=(jax.ShapeDtypeStruct((SLOTS, WIDTH), BF...  98.6 us
    pallas_call x1, Pallas kernels, body(): pl.pallas_call(finish, grid=(WIDTH // COLUMNS,), out_shape=(jax.ShapeDtyp...  3.56 us

profile of v4, /device:TPU:39, one launch (start us, length us, event | category | flops | bytes accessed | tf_op | source)
XLA Modules:
  0.0 104.7 jit_solution(4461820183759544704)
XLA Ops:
  2.6 98.6 %shard_map.94 = (bf16[768,1152]{1,0:T(8,128)(2,1)}, bf16[384,768]{1,0:T(8,128)(2,1)}, f32[1,384]{1,0:T(1,128)}, bf16[128,1152]{1,0:T(8,128)(2,1)}) custom-call(bf16[384,1152]{1,0:T(8,128)(2,1)} %img_hbm.1, bf16[128,1152]{1,0:T(8,128)(2,1)} %txt_hbm.1, s32[1,384]{1,0:T(1,128)} %bitcast.1, s32[384]{0:T(512)} %lab_ref.1, s32[1]{0:T(128)S(6)} %copy.10.cnt_ref, ...), custom_call_target="tpu_custom_call" | custom-call | tf_op jit(solution)/shard_map/pallas_call | solution.py:400
  101.2 3.6 %shard_map.95 = (bf16[384,1152]{1,0:T(8,128)(2,1)}, bf16[384]{0:T(512)(128)(2,1)}, bf16[128,1152]{1,0:T(8,128)(2,1)}) custom-call(bf16[768,1152]{1,0:T(8,128)(2,1)} %get-tuple-element.7.back_ref, bf16[384,768]{1,0:T(8,128)(2,1)} %get-tuple-element.8.pick_ref, f32[1,384]{1,0:T(1,128)} %get-tuple-element.9.losses_ref, bf16[128,1152]{1,0:T(8,128)(2,1)} %get-tuple-element.10.sums_ref), custom_call_target="tpu_custom_call" | custom-call | tf_op jit(solution)/shard_map/pallas_call | solution.py:450
